TPU v7x, 128 devices: a whole 4x4x4 slice. The times are simulated.
128 devices in a mesh: section: 2 (over core), dp: 8 (over y_lo, z), tensor: 8 (over x, y_hi).
Axes of the slice: x: 4, y: 4 (y_hi: 2, y_lo: 2; y = y_hi * 2 + y_lo), z: 4, core: 2. Of those that a mesh axis runs over, the one named last changes fastest.
Arguments:
- context: bfloat16 [2, 2048, 6144], P(None, 'dp', ('section', 'tensor')), may hold values from -6 to 6
- residual: bfloat16 [2, 2048, 9216], P(None, 'dp', ('section', 'tensor')), may hold values from -6 to 6
- out_weight: bfloat16 [6144, 9216], P(('section', 'tensor')), may hold values from -0.109375 to 0.109375
- out_bias: float32 [9216], P(('section', 'tensor')), may hold values from -3 to 3
- norm_gain: float32 [9216], replicated, may hold values from 0.1 to 1.9
- norm_bias: float32 [9216], replicated, may hold values from -3 to 3
- query_weight: bfloat16 [9216, 6144], P(None, 'tensor'), may hold values from -0.0625 to 0.0625
- query_bias: float32 [6144], P('tensor'), may hold values from -3 to 3
- grad_handoff: bfloat16 [2, 2048, 9216], P('section', ('dp', 'tensor')), may hold values from -16 to 16
Outputs:
- query: bfloat16 [2, 2048, 6144], P('section', 'dp', 'tensor')
- grad_context: bfloat16 [2, 2048, 6144], P(None, 'dp', ('section', 'tensor'))
- grad_out_weight: bfloat16 [6144, 9216], P(('section', 'tensor'), 'dp')
All inputs are finite; a program needn't handle non-finite values.
Results may differ from a plain program's by a relative error of at most 0.017.
Values may be sent and summed in bfloat16 or wider, within the bound.
A program may use at most 128 MiB of HBM per device.

v0:
```python
import jax
import jax.numpy as jnp
from jax import lax
from jax.sharding import PartitionSpec as P

epsilon = 1e-05


def layer_norm(values, norm_gain, norm_bias):
    wide = values.astype(jnp.float32)
    mean_value = jnp.mean(wide, axis=-1, keepdims=True)
    centred = wide - mean_value
    variance = jnp.mean(centred * centred, axis=-1, keepdims=True)
    return (centred * lax.rsqrt(variance + epsilon) * norm_gain + norm_bias).astype(jnp.bfloat16)


def local(
    context,
    residual,
    out_weight,
    out_bias,
    norm_gain,
    norm_bias,
    query_weight,
    query_bias,
    grad_handoff,
):
    seq_count, row_count, head_cols = context.shape
    width = out_weight.shape[1]
    flat_ctx = context.reshape(seq_count * row_count, head_cols)
    partial_value = jnp.dot(flat_ctx, out_weight, preferred_element_type=jnp.float32).reshape(
        seq_count, row_count, width
    )
    summed = lax.psum_scatter(
        partial_value.astype(jnp.bfloat16), ("section", "tensor"), scatter_dimension=2, tiled=True
    ).astype(jnp.float32)
    handoff = (residual.astype(jnp.float32) + summed + out_bias).astype(jnp.bfloat16)
    gathered = lax.all_gather(handoff, ("section", "tensor"), axis=2, tiled=True)
    own_seq = lax.dynamic_index_in_dim(gathered, lax.axis_index("section"), 0, keepdims=True)
    normed = layer_norm(own_seq, norm_gain, norm_bias)
    query_cols = query_weight.shape[1]
    query = (
        jnp.dot(normed.reshape(row_count, width), query_weight, preferred_element_type=jnp.float32)
        + query_bias
    )
    query = query.astype(jnp.bfloat16).reshape(1, row_count, query_cols)
    flat_rows = lax.all_gather(grad_handoff, ("section", "tensor"), axis=1, tiled=True).reshape(
        -1, width
    )
    back_rows = lax.dot_general(
        flat_rows, out_weight, (((1,), (1,)), ((), ())), preferred_element_type=jnp.float32
    )
    grad_ctx = back_rows
    weight_term = lax.dot_general(
        flat_ctx, flat_rows, (((0,), (0,)), ((), ())), preferred_element_type=jnp.float32
    )
    grad_ctx, weight_term = (grad_ctx, weight_term)
    grad_context = grad_ctx.astype(jnp.bfloat16).reshape(seq_count, row_count, head_cols)
    grad_out_weight = lax.psum_scatter(
        weight_term.astype(jnp.bfloat16), "dp", scatter_dimension=1, tiled=True
    )
    return (query, grad_context, grad_out_weight)


def solution(mesh):
    in_specs = (
        P(None, "dp", ("section", "tensor")),
        P(None, "dp", ("section", "tensor")),
        P(("section", "tensor"), None),
        P(("section", "tensor")),
        P(),
        P(),
        P(None, "tensor"),
        P("tensor"),
        P("section", ("dp", "tensor"), None),
    )
    out_specs = (
        P("section", "dp", "tensor"),
        P(None, "dp", ("section", "tensor")),
        P(("section", "tensor"), "dp"),
    )
    return jax.shard_map(local, mesh=mesh, in_specs=in_specs, out_specs=out_specs, check_vma=False)
```

profile of v0, /device:TPU:1, one launch (start us, length us, event | category | flops | bytes accessed | tf_op | source)
XLA Modules:
  0.0 386.6 jit_solution(13120774381191356858)
XLA Ops:
  7.2 0.0 copy-start
  7.2 0.0 all-gather.5.cloned.1.call-start
  7.2 0.7 all-gather.5.cloned.1.call-update
  7.9 0.0 reduce-scatter.5.cloned.1.call-start
  8.0 0.2 copy-done
  8.2 11.5 %convolution_convert_fusion = bf16[2,256,9216]{1,2,0:T(8,128)(2,1)} fusion(bf16[2,256,384]{2,1,0:T(8,128)(2,1)S(1)} %copy-done, bf16[384,9216]{1,0:T(8,128)(2,1)} %param.11), kind=kOutput, calls=%fused_computation | convolution fusion | flops 3628597248 | bytes 16908288 | tf_op jit(solution)/shard_map/dot_general | solution.py:31
  19.7 0.0 reduce-scatter.5.cloned.1.call-update
  19.7 0.0 reduce-scatter.7.cloned.1.call-start
  19.8 71.4 %all-gather.5.cloned.1.call-done = bf16[1,512,9216]{2,1,0:T(8,128)(2,1)} async-done(((bf16[1,32,9216]{2,1,0:T(8,128)(2,1)}), bf16[1,512,9216]{2,1,0:T(8,128)(2,1)}) %all-gather.5.cloned.1.call-update) | async-done | bytes 9437200 | tf_op jit(solution)/shard_map/all_gather | solution.py:47
  91.2 9.5 %convolution_convert_fusion.1 = bf16[384,9216]{1,0:T(8,128)(2,1)} fusion(bf16[512,384]{1,0:T(8,128)(2,1)S(1)} %bitcast.29, bf16[1,512,9216]{2,1,0:T(8,128)(2,1)} %all-gather.5.cloned.1.call-done), kind=kOutput, calls=%fused_computation.1 | convolution fusion | flops 3627417600 | bytes 16908288 | tf_op jit(solution)/shard_map/dot_general | solution.py:54
  100.6 0.0 copy-start.3
  100.6 0.0 copy-start.4
  100.6 11.0 %copy.16 = bf16[384,9216]{0,1:T(8,128)(2,1)} copy(bf16[384,9216]{1,0:T(8,128)(2,1)} %convolution_convert_fusion.1) | data formatting | bytes 14155776
  111.6 0.0 reduce-scatter.7.cloned.1.call-update
  111.6 0.0 all-gather.3.cloned.1.call-start
  111.7 87.5 %reduce-scatter.5.cloned.1.call-done = bf16[2,256,576]{1,2,0:T(8,128)(2,1)} async-done(((bf16[2,256,9216]{1,2,0:T(8,128)(2,1)}), bf16[2,256,576]{1,2,0:T(8,128)(2,1)}) %reduce-scatter.5.cloned.1.call-update) | async-done | bytes 589840 | tf_op jit(solution)/shard_map/reduce_scatter | solution.py:34
  199.1 0.0 copy-done.3
  199.1 0.0 copy-done.4
  199.1 2.1 add_convert_fusion
  201.2 0.0 all-gather.3.cloned.1.call-update
  201.2 10.4 %fusion.24 = bf16[512,384]{1,0:T(8,128)(2,1)} fusion(bf16[384,9216]{1,0:T(8,128)(2,1)} %param.11, bf16[1,512,9216]{2,1,0:T(8,128)(2,1)} %all-gather.5.cloned.1.call-done), kind=kOutput, calls=%fused_computation.23 | convolution fusion | flops 3624075264 | bytes 16908288 | tf_op jit(solution)/shard_map/dot_general | solution.py:50
  211.6 0.0 copy-start.5
  211.6 0.0 copy-start.6
  211.6 0.0 copy-start.7
  211.6 70.6 %reduce-scatter.7.cloned.1.call-done = bf16[1152,384]{1,0:T(8,128)(2,1)} async-done(((bf16[9216,384]{1,0:T(8,128)(2,1)}), bf16[1152,384]{1,0:T(8,128)(2,1)}) %reduce-scatter.7.cloned.1.call-update) | async-done | bytes 884752
  282.2 2.2 copy.17
  284.5 76.3 %all-gather.3.cloned.1.call-done = bf16[2,256,9216]{1,2,0:T(8,128)(2,1)} async-done(((bf16[2,256,576]{1,2,0:T(8,128)(2,1)}), bf16[2,256,9216]{1,2,0:T(8,128)(2,1)}) %all-gather.3.cloned.1.call-update) | async-done | bytes 9437200 | tf_op jit(solution)/shard_map/all_gather | solution.py:38
  360.8 0.0 copy-start.2
  360.8 3.1 convert_reduce_fusion
  364.0 3.6 fusion.2
  367.5 0.0 copy-done.5
  367.5 0.0 copy-done.6
  367.6 0.0 copy-done.7
  367.6 0.0 copy-done.2
  367.6 0.0 copy-start.1
  367.6 12.5 %fusion.27 = bf16[1,256,768]{2,1,0:T(8,128)(2,1)} fusion(bf16[9216,768]{1,0:T(8,128)(2,1)} %param.15, f32[9216]{0:T(1024)S(1)} %copy-done.5, f32[9216]{0:T(1024)S(1)} %copy-done.6, f32[256]{0:T(256)S(1)} %add_rsqrt_fusion, f32[256]{0:T(256)S(1)} %broadcast_multiply_fusion, bf16[2,256,9216]{1,2,0:T(8,128)(2,1)S(1)} %copy-done.2, s32[]{:T(128)S(6)} %select_n.4, ...), kind=kOutput, calls=%fused_computation.24 | convolution fusion | flops 3638427648 | bytes 19347460 | tf_op jit(solution)/shard_map/dot_general | solution.py:43
  380.0 0.0 copy-done.1
  (2 shorter events, 0.0 us)
Async XLA Ops:
  7.2 1.0 copy-start
  7.2 84.0 %all-gather.5.cloned.1.call-start = ((), (), s32[]{:S(2)}) async-start(), calls=%async_computation.4 | async-start | bytes 10027008 | tf_op jit(solution)/shard_map/all_gather | solution.py:47
  7.9 191.2 %reduce-scatter.5.cloned.1.call-start = ((), (), s32[]{:S(2)}) async-start(), calls=%async_computation.2 | async-start | bytes 10027008 | tf_op jit(solution)/shard_map/reduce_scatter | solution.py:34
  19.7 262.5 %reduce-scatter.7.cloned.1.call-start = ((), (), s32[]{:S(2)}) async-start(), calls=%async_computation.5 | async-start | bytes 7962624
  100.6 98.5 %copy-start.3 = (bf16[2,256,576]{1,2,0:T(8,128)(2,1)S(1)}, bf16[2,256,576]{1,2,0:T(8,128)(2,1)}, u32[]{:S(2)}) copy-start(bf16[2,256,576]{1,2,0:T(8,128)(2,1)} %param.10) | copy-start | bytes 1769476
  100.6 98.5 %copy-start.4 = (f32[576]{0:T(1024)S(1)}, f32[576]{0:T(1024)}, u32[]{:S(2)}) copy-start(f32[576]{0:T(1024)} %param.12) | copy-start | bytes 6916
  111.6 249.2 %all-gather.3.cloned.1.call-start = ((), (), s32[]{:S(2)}) async-start(), calls=%async_computation.3 | async-start | bytes 10027008 | tf_op jit(solution)/shard_map/all_gather | solution.py:38
  211.6 155.9 %copy-start.5 = (f32[9216]{0:T(1024)S(1)}, f32[9216]{0:T(1024)}, u32[]{:S(2)}) copy-start(f32[9216]{0:T(1024)} %param.14) | copy-start | bytes 110596
  211.6 155.9 %copy-start.6 = (f32[9216]{0:T(1024)S(1)}, f32[9216]{0:T(1024)}, u32[]{:S(2)}) copy-start(f32[9216]{0:T(1024)} %param.13) | copy-start | bytes 110596
  211.6 155.9 %copy-start.7 = (f32[768]{0:T(1024)S(1)}, f32[768]{0:T(1024)}, u32[]{:S(2)}) copy-start(f32[768]{0:T(1024)} %param.16) | copy-start | bytes 9220
  360.8 6.8 %copy-start.2 = (bf16[2,256,9216]{1,2,0:T(8,128)(2,1)S(1)}, bf16[2,256,9216]{1,2,0:T(8,128)(2,1)}, u32[]{:S(2)}) copy-start(bf16[2,256,9216]{1,2,0:T(8,128)(2,1)} %all-gather.3.cloned.1.call-done) | copy-start | bytes 28311556
  367.6 12.5 %copy-start.1 = (bf16[2,256,384]{2,1,0:T(8,128)(2,1)S(1)}, bf16[2,256,384]{2,1,0:T(8,128)(2,1)}, u32[]{:S(2)}) copy-start(bf16[2,256,384]{2,1,0:T(8,128)(2,1)} %param.9) | copy-start | bytes 1179652
Sparse Core Ops, SparseCore 0:
  10.4 80.6 all-gather.4
  95.6 103.5 reduce-scatter.4
  201.6 80.6 reduce-scatter.6
  284.7 76.0 all-gather.2
where the time goes:
time: 387 us
  waiting for transfers between devices  307 us (79%)
  matrix products  43.8 us (11%)
  between operations  13.8 us (4%)
  local copies, waits for them, and re-layouts  13.4 us (3%)
  other arithmetic  8.8 us (2%)
    reduce_scatter x1, waiting for transfers between devices, local(): lax.psum_scatter(partial_value.astype(jnp.bfloat16), ('section', 'tensor'...  87.5 us
    all_gather x1, waiting for transfers between devices, local(): lax.all_gather(handoff, ('section', 'tensor'), axis=2, tiled=True)  76.3 us
    all_gather x1, waiting for transfers between devices, local(): lax.all_gather(grad_handoff, ('section', 'tensor'), axis=1, tiled=True)  71.4 us
    unnamed x5, waiting for transfers between devices  71.3 us
    unnamed x18, local copies, waits for them, and re-layouts  13.4 us
    dot_general x1, matrix products, local(): jnp.dot(normed.reshape(row_count, width), query_weight, preferred_element...  12.5 us
    dot_general x1, matrix products, local(): jnp.dot(flat_ctx, out_weight, preferred_element_type=jnp.float32)  11.5 us
    dot_general x1, matrix products, local(): lax.dot_general(flat_rows, out_weight, (((1,), (1,)), ((), ())), preferre...  10.4 us
  transfers between devices with their start and end apart: 4, of which 4 were waited for; matrix products, arithmetic and copies ran while one was open for 12% of the time, Pallas kernels for 0%

commit v1 on v0

v1 whole, which is shorter than its diff:
```python
import jax
import jax.numpy as jnp
from jax import lax
from jax.experimental import pallas as pl
from jax.experimental.pallas import tpu as pltpu
from jax.sharding import PartitionSpec as P

EPSILON = 1e-05
MESH = pl.DeviceIdType.MESH
BF16 = jnp.bfloat16
F32 = jnp.float32

CHUNKS = 8
CW = 1152
WIDTH = CHUNKS * CW
SEQ_ROWS = 256
PIECE = 32
HEADS = 384
HALF = HEADS // 2
QCOLS = 768
WQ_SLOTS = 3

STAGES = {
    "g1": (0, 2),
    "p1": (0, 1),
    "p2": (1, 1),
    "p3": (3, 1),
    "p4": (5, 1),
    "p5": (7, 1),
    "g2": (2, 2),
    "g3": (3, 2),
    "g4": (5, 2),
    "c": (6, 2),
    "w2": (8, 2),
    "n2": (15, 1),
    "n3": (16, 1),
    "q": (18, 1),
}
LN_TICK = 14
TICKS = 26


def wait_for(ref, sem):
    pltpu.make_async_copy(ref, ref, sem).wait()


def kernel(
    ctx_hbm, res_hbm, ow_hbm, bias_ref, gain_ref, nbias_ref, qw_hbm, qbias_ref, grad_hbm,
    query_ref, gctx_ref, gow_ref,
    ctx, ctxt, res, wv, xsend, xbuf, pbuf, s1r, s1l, finl, finr, ybuf, hbuf,
    wq, gbuf, wbuf, ws1r, ws1l, wfinl, wfinr, wy, gacc, qacc, rowsum,
    in_sem, wv_sem, wq_sem, gin_sem,
    xsend_sem, xrecv_sem, p_send, s1r_sem, s1l_sem, finl_sem, finr_sem, y_sem,
    g_send, gc_send, g_sem, gc_sem, n_send, n_sem,
    w_send, ws1_send, ws1r_sem, ws1l_sem, wfinl_sem, wfinr_sem, wy_send, wy_sem,
):
    s = lax.axis_index("section")
    d = lax.axis_index("dp")
    t = lax.axis_index("tensor")
    x, yh = t // 2, t % 2
    yl, z = d // 4, d % 4
    other_core = (1 - s, d, t)
    xr = (s, d, ((x + 1) % 4) * 2 + yh)
    xl = (s, d, ((x + 3) % 4) * 2 + yh)
    ypart = (s, d, x * 2 + (1 - yh))
    zr = (s, yl * 4 + (z + 1) % 4, t)
    zl = (s, yl * 4 + (z + 3) % 4, t)
    pair = (s, (1 - yl) * 4 + z, t)

    def send(src, dst, ssem, rsem, to):
        pltpu.make_async_remote_copy(
            src_ref=src, dst_ref=dst, send_sem=ssem, recv_sem=rsem, device_id=to, device_id_type=MESH
        ).start()

    def own_rows(offset):
        return pl.ds(((x + offset) % 4) * 64 + yh * PIECE, PIECE)

    def far_rows(offset):
        return pl.ds(((x + offset) % 4) * 64 + (1 - yh) * PIECE, PIECE)

    ctx_load = pltpu.make_async_copy(ctx_hbm, ctx, in_sem.at[0])
    ctx_load.start()

    def wv_load(c):
        return pltpu.make_async_copy(
            ow_hbm.at[:, pl.ds(pl.multiple_of(c * CW, 128), CW)], wv.at[c], wv_sem.at[c]
        )

    def gin_load(c):
        return pltpu.make_async_copy(
            grad_hbm.at[:, pl.ds(pl.multiple_of(c * CW, 128), CW)],
            gbuf.at[c, pl.ds(s * SEQ_ROWS + t * PIECE, PIECE)],
            gin_sem.at[c],
        )

    def wq_load(c):
        return pltpu.make_async_copy(
            qw_hbm.at[pl.ds(c * CW, CW)], wq.at[c % WQ_SLOTS], wq_sem.at[c % WQ_SLOTS]
        )

    wv_load(0).start()

    @pl.loop(0, CHUNKS)
    def _(c):
        gin_load(c).start()

    res_load = pltpu.make_async_copy(res_hbm, res, in_sem.at[1])
    res_load.start()

    @pl.loop(1, CHUNKS)
    def _(c):
        wv_load(c).start()

    @pl.loop(0, WQ_SLOTS)
    def _(c):
        wq_load(c).start()

    barrier = pltpu.get_barrier_semaphore()
    neighbours = (other_core, xr, xl, ypart, zr, zl, pair)
    for to in neighbours:
        pl.semaphore_signal(barrier, inc=1, device_id=to, device_id_type=MESH)

    ctx_load.wait()
    ctxt[...] = ctx[...].T
    gacc[...] = jnp.zeros_like(gacc)
    qacc[...] = jnp.zeros_like(qacc)
    rowsum[...] = jnp.zeros_like(rowsum)
    res_load.wait()

    @pl.loop(0, CHUNKS)
    def _(c):
        gin_load(c).wait()

    pl.semaphore_wait(barrier, len(neighbours))

    res_chunk = 4 * s + x

    def p1(c):
        slot = c % 2

        @pl.when(c < 4)
        def _():
            wv_load(c).wait()

        @pl.when(c == 4)
        def _():
            for later in range(4, CHUNKS):
                wv_load(later).wait()

        @pl.when(c >= 2)
        def _():
            wait_for(xsend.at[slot], xsend_sem.at[slot])

        rows = pl.ds((1 - s) * SEQ_ROWS, SEQ_ROWS)
        part = jnp.dot(ctx[rows], wv[c], preferred_element_type=F32)

        @pl.when(c == res_chunk)
        def _():
            xsend[slot] = (part + res[rows].astype(F32) + bias_ref[...]).astype(BF16)

        @pl.when(c != res_chunk)
        def _():
            xsend[slot] = part.astype(BF16)

        send(xsend.at[slot], xbuf.at[c], xsend_sem.at[slot], xrecv_sem.at[c], other_core)

    def p2(c):
        rows = pl.ds(s * SEQ_ROWS, SEQ_ROWS)
        part = jnp.dot(ctx[rows], wv[c], preferred_element_type=F32)
        wait_for(xbuf.at[c], xrecv_sem.at[c])

        @pl.when(c == res_chunk)
        def _():
            pbuf[c] = (part + xbuf[c].astype(F32) + res[rows].astype(F32) + bias_ref[...]).astype(BF16)

        @pl.when(c != res_chunk)
        def _():
            pbuf[c] = (part + xbuf[c].astype(F32)).astype(BF16)

        send(pbuf.at[c, far_rows(2)], s1r.at[c], p_send, s1r_sem.at[c], xr)
        send(pbuf.at[c, own_rows(2)], s1l.at[c], p_send, s1l_sem.at[c], xl)
        send(pbuf.at[c, own_rows(1)], finl.at[c, 0], p_send, finl_sem.at[c, 0], xr)
        send(pbuf.at[c, far_rows(3)], finr.at[c, 1], p_send, finr_sem.at[c, 1], xl)

    def p3(c):
        wait_for(s1r.at[c], s1r_sem.at[c])
        rows = far_rows(1)
        pbuf[c, rows] = (pbuf[c, rows].astype(F32) + s1r[c].astype(F32)).astype(BF16)
        send(pbuf.at[c, rows], finl.at[c, 1], p_send, finl_sem.at[c, 1], xr)
        wait_for(s1l.at[c], s1l_sem.at[c])
        rows = own_rows(3)
        pbuf[c, rows] = (pbuf[c, rows].astype(F32) + s1l[c].astype(F32)).astype(BF16)
        send(pbuf.at[c, rows], finr.at[c, 0], p_send, finr_sem.at[c, 0], xl)

    def p4(c):
        wait_for(finl.at[c, 1], finl_sem.at[c, 1])
        wait_for(finr.at[c, 1], finr_sem.at[c, 1])
        rows = far_rows(0)
        pbuf[c, rows] = (
            pbuf[c, rows].astype(F32) + finl[c, 1].astype(F32) + finr[c, 1].astype(F32)
        ).astype(BF16)
        send(pbuf.at[c, rows], ybuf.at[c], p_send, y_sem.at[c], ypart)

    def p5(c):
        wait_for(finl.at[c, 0], finl_sem.at[c, 0])
        wait_for(finr.at[c, 0], finr_sem.at[c, 0])
        wait_for(ybuf.at[c], y_sem.at[c])
        total = (
            pbuf[c, own_rows(0)].astype(F32)
            + finl[c, 0].astype(F32)
            + finr[c, 0].astype(F32)
            + ybuf[c].astype(F32)
        )
        handoff = total.astype(BF16)
        hbuf[c] = handoff
        rowsum[...] += jnp.sum(handoff.astype(F32), axis=-1, keepdims=True)

    def gather1(buf, c, base, sems, ssem):
        rows = own_rows(0)
        rows = pl.ds(base + rows.start, PIECE)
        send(buf.at[c, rows], buf.at[c, rows], ssem, sems.at[c, 0], ypart)
        send(buf.at[c, rows], buf.at[c, rows], ssem, sems.at[c, 1], xr)
        send(buf.at[c, rows], buf.at[c, rows], ssem, sems.at[c, 2], xl)

    def shifted(rows, base):
        return pl.ds(base + rows.start, PIECE)

    def gather2(buf, c, base, sems, ssem):
        rows = shifted(own_rows(3), base)
        wait_for(buf.at[c, rows], sems.at[c, 1])
        send(buf.at[c, rows], buf.at[c, rows], ssem, sems.at[c, 5], xr)
        rows = shifted(far_rows(0), base)
        wait_for(buf.at[c, rows], sems.at[c, 0])
        send(buf.at[c, rows], buf.at[c, rows], ssem, sems.at[c, 4], xl)
        send(buf.at[c, rows], buf.at[c, rows], ssem, sems.at[c, 3], xr)

    def gather3(buf, c, base, sems, ssem):
        rows = shifted(far_rows(1), base)
        wait_for(buf.at[c, rows], sems.at[c, 4])
        send(buf.at[c, rows], buf.at[c, rows], ssem, sems.at[c, 6], xl)

    def gather4(buf, c, base, sems):
        wait_for(buf.at[c, shifted(own_rows(1), base)], sems.at[c, 2])
        wait_for(buf.at[c, shifted(far_rows(3), base)], sems.at[c, 3])
        wait_for(buf.at[c, shifted(own_rows(2), base)], sems.at[c, 5])
        wait_for(buf.at[c, shifted(far_rows(2), base)], sems.at[c, 6])

    def order(j):
        near = j % 2
        ring = (j + 2) // 4
        mid = ring % 2
        step = (2 + ring * (3 + 2 * near)) % 4
        own = near + mid * ((j + 2) // 2 - 2 - near)
        half = (yl + 1 + own) % 2
        return half * 4 + (z + step) % 4, own

    g_base = s * SEQ_ROWS

    def g1(j):
        gather1(gbuf, order(j)[0], g_base, g_sem, g_send)

    def g2(j):
        gather2(gbuf, order(j)[0], g_base, g_sem, g_send)

    def g3(j):
        gather3(gbuf, order(j)[0], g_base, g_sem, g_send)

    def g4(j):
        c = order(j)[0]
        gather4(gbuf, c, g_base, g_sem)
        rows = pl.ds(g_base, SEQ_ROWS)
        send(gbuf.at[c, rows], gbuf.at[c, rows], gc_send, gc_sem.at[c], other_core)

    def compute(j):
        c, own = order(j)
        rows = pl.ds((1 - s) * SEQ_ROWS, SEQ_ROWS)
        wait_for(gbuf.at[c, rows], gc_sem.at[c])
        slot = j % 6

        @pl.when(j >= 6)
        def _():
            wait_for(wbuf.at[slot], ws1_send.at[slot])

        term = jnp.dot(ctxt[...], gbuf[c], preferred_element_type=F32).astype(BF16)
        wbuf[slot, 0] = term[:HALF]
        wbuf[slot, 1] = term[HALF:]

        @pl.when(j < 2)
        def _():
            send(wbuf.at[slot, 0], ws1r.at[own], ws1_send.at[slot], ws1r_sem.at[own], zr)
            send(wbuf.at[slot, 1], ws1l.at[own], ws1_send.at[slot], ws1l_sem.at[own], zl)

        @pl.when((j >= 2) & (j < 6) & (j % 2 == 0))
        def _():
            send(wbuf.at[slot, 1], wfinl.at[own, 1], w_send, wfinl_sem.at[own, 1], zr)

        @pl.when((j >= 2) & (j < 6) & (j % 2 == 1))
        def _():
            send(wbuf.at[slot, 0], wfinr.at[own, 0], w_send, wfinr_sem.at[own, 0], zl)

        gacc[...] += lax.dot_general(
            gbuf[c], wv[c], (((1,), (1,)), ((), ())), preferred_element_type=F32
        )

    def w2(j):
        own = order(j)[1]

        @pl.when((j >= 2) & (j < 6) & (j % 2 == 0))
        def _():
            wait_for(ws1r.at[own], ws1r_sem.at[own])
            wbuf[j, 0] = (wbuf[j, 0].astype(F32) + ws1r[own].astype(F32)).astype(BF16)
            send(wbuf.at[j, 0], wfinl.at[own, 0], w_send, wfinl_sem.at[own, 0], zr)

        @pl.when((j >= 2) & (j < 6) & (j % 2 == 1))
        def _():
            wait_for(ws1l.at[own], ws1l_sem.at[own])
            wbuf[j, 1] = (wbuf[j, 1].astype(F32) + ws1l[own].astype(F32)).astype(BF16)
            send(wbuf.at[j, 1], wfinr.at[own, 1], w_send, wfinr_sem.at[own, 1], zl)

    def norm():
        mean = rowsum[...] * (1.0 / WIDTH)

        def square(c, total):
            centred = hbuf[c].astype(F32) - mean
            return total + jnp.sum(centred * centred, axis=-1, keepdims=True)

        total = lax.fori_loop(0, CHUNKS, square, jnp.zeros((PIECE, 1), F32))
        scale = lax.rsqrt(total * (1.0 / WIDTH) + EPSILON)

        @pl.loop(0, CHUNKS)
        def _(c):
            centred = hbuf[c].astype(F32) - mean
            gain = gain_ref[pl.ds(c, 1), :]
            shift = nbias_ref[pl.ds(c, 1), :]
            xbuf[c, own_rows(0)] = (centred * scale * gain + shift).astype(BF16)
            gather1(xbuf, c, 0, n_sem, n_send)

    def n2(c):
        gather2(xbuf, c, 0, n_sem, n_send)

    def n3(c):
        gather3(xbuf, c, 0, n_sem, n_send)

    def q(c):
        gather4(xbuf, c, 0, n_sem)
        wq_load(c).wait()
        qacc[...] += jnp.dot(xbuf[c], wq[c % WQ_SLOTS], preferred_element_type=F32)

        @pl.when(c + WQ_SLOTS < CHUNKS)
        def _():
            wq_load(c + WQ_SLOTS).start()

    bodies = {
        "g1": g1, "p1": p1, "p2": p2, "p3": p3, "p4": p4, "p5": p5, "g2": g2, "g3": g3, "g4": g4,
        "c": compute, "w2": w2, "n2": n2, "n3": n3, "q": q,
    }

    @pl.loop(0, TICKS)
    def _(k):
        for name, (first, stride) in STAGES.items():
            if name == "n2":

                @pl.when(k == LN_TICK)
                def _():
                    norm()

            index = (k - first) // stride

            @pl.when((k >= first) & (k < first + CHUNKS * stride) & ((k - first) % stride == 0))
            def _():
                bodies[name](index)

    gctx_ref[...] = gacc[...].astype(BF16)
    query_ref[...] = (qacc[...] + qbias_ref[...]).astype(BF16)

    for half in range(2):
        wait_for(wfinl.at[0, half], wfinl_sem.at[0, half])
        wait_for(wfinr.at[0, half], wfinr_sem.at[0, half])
        wbuf[0, half] = (
            wbuf[0, half].astype(F32) + wfinl[0, half].astype(F32) + wfinr[0, half].astype(F32)
        ).astype(BF16)
        send(wbuf.at[0, half], wy.at[half], wy_send.at[half], wy_sem.at[half], pair)
    for half in range(2):
        wait_for(wfinl.at[1, half], wfinl_sem.at[1, half])
        wait_for(wfinr.at[1, half], wfinr_sem.at[1, half])
        wait_for(wy.at[half], wy_sem.at[half])
        gow_ref[half] = (
            wbuf[1, half].astype(F32)
            + wfinl[1, half].astype(F32)
            + wfinr[1, half].astype(F32)
            + wy[half].astype(F32)
        ).astype(BF16)

    for slot in range(2):
        wait_for(xsend.at[slot], xsend_sem.at[slot])
        wait_for(wy.at[slot], wy_send.at[slot])
    wait_for(pbuf.at[:, pl.ds(0, 224)], p_send)
    wait_for(gbuf.at[:, pl.ds(0, 224)], g_send)
    wait_for(gbuf.at[:, pl.ds(0, 256)], gc_send)
    wait_for(xbuf.at[:, pl.ds(0, 224)], n_send)
    wait_for(wbuf.at[pl.ds(2, 4)], w_send)


def local(
    context, residual, out_weight, out_bias, norm_gain, norm_bias, query_weight, query_bias, grad_handoff
):
    t = lax.axis_index("tensor")
    rows = 2 * SEQ_ROWS
    feats = WIDTH // 16
    ctx = context.reshape(rows, HEADS)
    res = residual.reshape(rows, feats)
    even = t % 2 == 0

    def place(a):
        zero = jnp.zeros_like(a)
        return jnp.where(
            even, jnp.concatenate([a, zero], axis=1), jnp.concatenate([zero, a], axis=1)
        )

    dma = pltpu.SemaphoreType.DMA
    any_spec = pl.BlockSpec(memory_space=pl.ANY)
    vmem_spec = pl.BlockSpec(memory_space=pltpu.VMEM)
    query, gctx, gow = pl.pallas_call(
        kernel,
        out_shape=(
            jax.ShapeDtypeStruct((SEQ_ROWS, QCOLS), BF16),
            jax.ShapeDtypeStruct((rows, HEADS), BF16),
            jax.ShapeDtypeStruct((2, HALF, CW), BF16),
        ),
        in_specs=[any_spec, any_spec, any_spec, vmem_spec, vmem_spec, vmem_spec, any_spec, vmem_spec, any_spec],
        out_specs=(vmem_spec, vmem_spec, vmem_spec),
        scratch_shapes=[
            pltpu.VMEM((rows, HEADS), BF16),
            pltpu.VMEM((HEADS, rows), BF16),
            pltpu.VMEM((rows, CW), BF16),
            pltpu.VMEM((CHUNKS, HEADS, CW), BF16),
            pltpu.VMEM((2, SEQ_ROWS, CW), BF16),
            pltpu.VMEM((CHUNKS, SEQ_ROWS, CW), BF16),
            pltpu.VMEM((CHUNKS, SEQ_ROWS, CW), BF16),
            pltpu.VMEM((CHUNKS, PIECE, CW), BF16),
            pltpu.VMEM((CHUNKS, PIECE, CW), BF16),
            pltpu.VMEM((CHUNKS, 2, PIECE, CW), BF16),
            pltpu.VMEM((CHUNKS, 2, PIECE, CW), BF16),
            pltpu.VMEM((CHUNKS, PIECE, CW), BF16),
            pltpu.VMEM((CHUNKS, PIECE, CW), BF16),
            pltpu.VMEM((WQ_SLOTS, CW, QCOLS), BF16),
            pltpu.VMEM((CHUNKS, rows, CW), BF16),
            pltpu.VMEM((6, 2, HALF, CW), BF16),
            pltpu.VMEM((2, HALF, CW), BF16),
            pltpu.VMEM((2, HALF, CW), BF16),
            pltpu.VMEM((2, 2, HALF, CW), BF16),
            pltpu.VMEM((2, 2, HALF, CW), BF16),
            pltpu.VMEM((2, HALF, CW), BF16),
            pltpu.VMEM((rows, HEADS), F32),
            pltpu.VMEM((SEQ_ROWS, QCOLS), F32),
            pltpu.VMEM((PIECE, 1), F32),
            dma((2,)),
            dma((CHUNKS,)),
            dma((WQ_SLOTS,)),
            dma((CHUNKS,)),
            dma((2,)),
            dma((CHUNKS,)),
            dma,
            dma((CHUNKS,)),
            dma((CHUNKS,)),
            dma((CHUNKS, 2)),
            dma((CHUNKS, 2)),
            dma((CHUNKS,)),
            dma,
            dma,
            dma((CHUNKS, 7)),
            dma((CHUNKS,)),
            dma,
            dma((CHUNKS, 7)),
            dma,
            dma((2,)),
            dma((2,)),
            dma((2,)),
            dma((2, 2)),
            dma((2, 2)),
            dma((2,)),
            dma((2,)),
        ],
        compiler_params=pltpu.CompilerParams(
            collective_id=0, has_side_effects=True, vmem_limit_bytes=62 * 2**20
        ),
    )(
        ctx,
        place(res),
        out_weight,
        place(out_bias.reshape(1, feats)),
        norm_gain.reshape(CHUNKS, CW),
        norm_bias.reshape(CHUNKS, CW),
        query_weight,
        query_bias.reshape(1, QCOLS),
        grad_handoff.reshape(PIECE, WIDTH),
    )
    return (
        query.reshape(1, SEQ_ROWS, QCOLS),
        gctx.reshape(2, SEQ_ROWS, HEADS),
        gow.reshape(HEADS, CW),
    )


def solution(mesh):
    in_specs = (
        P(None, "dp", ("section", "tensor")),
        P(None, "dp", ("section", "tensor")),
        P(("section", "tensor"), None),
        P(("section", "tensor")),
        P(),
        P(),
        P(None, "tensor"),
        P("tensor"),
        P("section", ("dp", "tensor"), None),
    )
    out_specs = (
        P("section", "dp", "tensor"),
        P(None, "dp", ("section", "tensor")),
        P(("section", "tensor"), "dp"),
    )
    return jax.shard_map(local, mesh=mesh, in_specs=in_specs, out_specs=out_specs, check_vma=False)
```

time: 387 us -> 168 us (0.43)
  waiting for transfers between devices: 307 us -> 0 us
  Pallas kernels: 0 us -> 154 us
  matrix products: 43.8 us -> 0 us
  between operations: 13.8 us -> 0.67 us
  other arithmetic: 8.8 us -> 2.14 us
    pallas_call x0 -> x1, Pallas kernels: none -> 154 us  [local(): pl.pallas_call(kernel, out_shape=(jax.ShapeDtypeStruct((SEQ_ROWS, QCOLS),...]
    all_gather x2 -> x0, waiting for transfers between devices: 148 us -> none  [the longest x1 76.3 us: local(): lax.all_gather(handoff, ('section', 'tensor'), axis=2, tiled=True)]
    reduce_scatter x1 -> x0, waiting for transfers between devices: 87.5 us -> none  [local(): lax.psum_scatter(partial_value.astype(jnp.bfloat16), ('section', 'tensor'...]
    unnamed x5 -> x0, waiting for transfers between devices: 71.3 us -> none
    dot_general x4 -> x0, matrix products: 43.8 us -> none  [the longest x1 12.5 us: local(): jnp.dot(normed.reshape(row_count, width), query_weight, preferred_element...]
    unnamed x18 -> x6, local copies, waits for them, and re-layouts: 13.4 us -> 5.9 us
    reduce_sum x2 -> x0, other arithmetic: 6.71 us -> none  [the longest x1 3.57 us: layer_norm(): variance = jnp.mean(centred * centred, axis=-1, keepdims=True)]
    reshape x0 -> x4, local copies, waits for them, and re-layouts: none -> 4.75 us  [the longest x1 1.39 us: local(): norm_gain.reshape(CHUNKS, CW)]
  transfers between devices with their start and end apart: 4 -> 0, of which waited for: 4 -> 0; matrix products, arithmetic and copies ran while one was open for 12% -> 0% of each run, Pallas kernels for 0% -> 0%
where the time goes in v1:
time: 168 us; the launch traced here: 167 us
  Pallas kernels  154 us (92%)
  local copies, waits for them, and re-layouts  10.6 us (6%)
  other arithmetic  2.14 us (1%)
    pallas_call x1, Pallas kernels, local(): pl.pallas_call(kernel, out_shape=(jax.ShapeDtypeStruct((SEQ_ROWS, QCOLS),...  154 us
    unnamed x6, local copies, waits for them, and re-layouts  5.9 us

profile of v1, /device:TPU:1, one launch (start us, length us, event | category | flops | bytes accessed | tf_op | source)
XLA Modules:
  0.0 167.1 jit_solution(5849165681339889782)
XLA Ops:
  0.6 0.7 reshape.38
  1.3 0.7 broadcast_select_fusion.bias_ref
  2.0 1.3 reshape.41.qbias_ref
  3.3 1.4 reshape.39.gain_ref
  4.7 1.4 reshape.40.nbias_ref
  6.1 1.4 copy.12
  7.4 1.5 pad_select_fusion.res_hbm
  8.9 153.6 %shard_map.112 = (bf16[256,768]{1,0:T(8,128)(2,1)}, bf16[512,384]{1,0:T(8,128)(2,1)}, bf16[2,192,1152]{2,1,0:T(8,128)(2,1)}) custom-call(bf16[512,384]{1,0:T(8,128)(2,1)} %bitcast.11, bf16[512,1152]{1,0:T(8,128)(2,1)} %pad_select_fusion.res_hbm, bf16[384,9216]{1,0:T(8,128)(2,1)} %ow_hbm.1, f32[1,1152]{1,0:T(1,128)} %broadcast_select_fusion.bias_ref, ...), custom_call_target="tpu_custom_call" | custom-call | tf_op jit(solution)/shard_map/pallas_call | solution.py:423
  162.5 0.0 copy-start
  162.5 1.8 %copy.16 = bf16[1,256,768]{2,1,0:T(8,128)(2,1)} copy(bf16[1,256,768]{2,1,0:T(8,128)(2,1)} %bitcast.10) | data formatting | bytes 786432
  164.4 1.8 %copy.17 = bf16[2,256,384]{2,1,0:T(8,128)(2,1)} copy(bf16[2,256,384]{2,1,0:T(8,128)(2,1)} %bitcast.9) | data formatting | bytes 786432
  166.2 0.0 copy-done
  166.2 0.9 copy.18
Async XLA Ops:
  162.5 3.6 %copy-start = (bf16[2,192,1152]{2,1,0:T(8,128)(2,1)S(1)}, bf16[2,192,1152]{2,1,0:T(8,128)(2,1)}, u32[]{:S(2)}) copy-start(bf16[2,192,1152]{2,1,0:T(8,128)(2,1)} %get-tuple-element.8) | copy-start | bytes 2654212

commit v2 on v0

v2 whole, which is shorter than its diff:
```python
import jax
import jax.numpy as jnp
from jax import lax
from jax.experimental import pallas as pl
from jax.experimental.pallas import tpu as pltpu
from jax.sharding import PartitionSpec as P

EPSILON = 1e-05
MESH = pl.DeviceIdType.MESH
BF16 = jnp.bfloat16
F32 = jnp.float32

CHUNKS = 8
CW = 1152
WIDTH = CHUNKS * CW
FEATS = WIDTH // 16
SEQ_ROWS = 256
PIECE = 32
SUB = 16
UNITS = 8
HEADS = 384
HALF = HEADS // 2
QCOLS = 768
WQ_SLOTS = 2

SCHEDULE = {
    "g1": (0, 1, 2, 3, 4, 5, 6, 7),
    "c": (20, 21, 27, 29, 31, 37, 38, 44),
    "n2": (38, 39, 40, 41, 45, 46, 47, 49),
    "p3": (11, 13, 15, 19, 20, 23, 28, 32),
    "norm": (33, 42),
    "g3": (13, 14, 16, 17, 22, 27, 31, 36),
    "p1": (3, 4, 5, 6, 7, 8, 9, 10),
    "p5": (19, 23, 27, 32, 33, 34, 40, 41),
    "p4": (14, 18, 21, 26, 27, 30, 34, 37),
    "p2": (5, 9, 11, 13, 14, 18, 22, 25),
    "g2": (9, 10, 11, 12, 15, 20, 23, 29),
    "g4": (17, 18, 23, 24, 28, 34, 35, 41),
    "n3": (41, 42, 43, 44, 49, 50, 51, 52),
    "q": (44, 46, 47, 48, 52, 53, 54, 55),
    "w3": (44,),
    "w2": (20, 22, 27, 29, 32, 37, 38, 44),
}
G_XFIRST = (1, 1, 1, 1, 1, 1, 1, 0)
N_XFIRST = (1, 0, 0, 0, 0, 0, 0, 0)
SPAN = 30

RING_STEPS = (2, 2, 1, 3, 0, 1, 3, 0)
OWN_HALF = (0, 1, 0, 0, 0, 1, 1, 1)


def digit(table, j):
    packed = sum(v * 4**i for i, v in enumerate(table))
    scale = (1 + 3 * (j % 2)) * (1 + 15 * ((j // 2) % 2)) * (1 + 255 * (j // 4))
    return (packed // scale) % 4


def wait_for(ref, sem):
    pltpu.make_async_copy(ref, ref, sem).wait()


def kernel(
    ctx_hbm, res_hbm, ow_hbm, bias_hbm, gain_hbm, nbias_hbm, qw_hbm, qbias_hbm, grad_hbm,
    query_hbm, gctx_hbm, gow_hbm,
    ctx, ctxp, ctxt, rest, res, bias, gain, nbias, qbias, wv, xsend, xbuf, pbuf,
    s1r, s1l, finl, finr, ybuf, hbuf,
    wq, gbuf, wbuf, ws1r, ws1l, wfinl, wfinr, wy, gacc, qacc, rowsum, gctx, query,
    in_sem, wv_sem, wq_sem, gin_sem, out_sem,
    xsend_sem, xrecv_sem, p_send, s1r_sem, s1l_sem, finl_sem, finr_sem, y_sem,
    g_send, gc_send, g_sem, gc_sem, n_send, n_sem,
    w_send, ws1_send, ws1r_sem, ws1l_sem, wfinl_sem, wfinr_sem, wy_send, wy_sem,
):
    s = lax.axis_index("section")
    d = lax.axis_index("dp")
    t = lax.axis_index("tensor")
    x, yh = t // 2, t % 2
    yl, z = d // 4, d % 4
    other_core = (1 - s, d, t)
    xr = (s, d, ((x + 1) % 4) * 2 + yh)
    xl = (s, d, ((x + 3) % 4) * 2 + yh)
    ypart = (s, d, x * 2 + (1 - yh))
    zr = (s, yl * 4 + (z + 1) % 4, t)
    zl = (s, yl * 4 + (z + 3) % 4, t)
    pair = (s, (1 - yl) * 4 + z, t)

    def send(src, dst, ssem, rsem, to):
        pltpu.make_async_remote_copy(
            src_ref=src, dst_ref=dst, send_sem=ssem, recv_sem=rsem, device_id=to, device_id_type=MESH
        ).start()

    def own(offset):
        return ((x + offset) % 4) * 2 + yh

    def far(offset):
        return ((x + offset) % 4) * 2 + 1 - yh

    small = [
        pltpu.make_async_copy(ctx_hbm, ctx, in_sem.at[0]),
        pltpu.make_async_copy(gain_hbm, gain, in_sem.at[1]),
        pltpu.make_async_copy(nbias_hbm, nbias, in_sem.at[2]),
        pltpu.make_async_copy(qbias_hbm, qbias, in_sem.at[3]),
        pltpu.make_async_copy(bias_hbm, bias, in_sem.at[4]),
    ] + [
        pltpu.make_async_copy(
            res_hbm.at[q],
            rest.at[q, pl.ds(pl.multiple_of(yh * FEATS, 16), FEATS)],
            in_sem.at[5 + q],
        )
        for q in range(2)
    ]
    rest[...] = jnp.zeros_like(rest)
    for load in small:
        load.start()

    def wv_load(c):
        return pltpu.make_async_copy(
            ow_hbm.at[:, pl.ds(pl.multiple_of(c * CW, 128), CW)], wv.at[c], wv_sem.at[c]
        )

    def gin_load(c):
        return pltpu.make_async_copy(
            grad_hbm.at[:, pl.ds(pl.multiple_of(c * CW, 128), CW)],
            gbuf.at[c, pl.ds(s * SEQ_ROWS + t * PIECE, PIECE)],
            gin_sem.at[c],
        )

    def wq_load(c):
        return pltpu.make_async_copy(
            qw_hbm.at[pl.ds((c % 4) * 2 * CW, 2 * CW)], wq.at[c % WQ_SLOTS], wq_sem.at[c % WQ_SLOTS]
        )

    wv_load(0).start()

    @pl.loop(0, CHUNKS)
    def _(c):
        gin_load(c).start()

    @pl.loop(1, CHUNKS)
    def _(c):
        wv_load(c).start()

    @pl.loop(0, WQ_SLOTS)
    def _(c):
        wq_load(c).start()

    barrier = pltpu.get_barrier_semaphore()
    neighbours = (other_core, xr, xl, ypart, zr, zl, pair)
    for to in neighbours:
        pl.semaphore_signal(barrier, inc=1, device_id=to, device_id_type=MESH)

    gacc[...] = jnp.zeros_like(gacc)
    qacc[...] = jnp.zeros_like(qacc)
    rowsum[...] = jnp.zeros_like(rowsum)
    for load in small:
        load.wait()
    ctxt[...] = ctx[...].T
    for q in range(2):
        by_row = rest[q].T
        for t_ in range(8):
            for h in range(2):
                rows = slice(t_ * PIECE + h * SUB, t_ * PIECE + (h + 1) * SUB)
                ctxp[q, h, t_ * SUB:(t_ + 1) * SUB] = ctx[q * SEQ_ROWS + rows.start:q * SEQ_ROWS + rows.stop]
                res[q, h, t_ * SUB:(t_ + 1) * SUB] = by_row[rows]

    @pl.loop(0, CHUNKS)
    def _(c):
        gin_load(c).wait()

    pl.semaphore_wait(barrier, len(neighbours))

    res_chunk = 4 * s + x

    def pair_of(u):
        return u // 4, pl.ds((u % 4) * 2, 2)

    def product(q, u, finish):
        h = u // 4
        for i in range(2):
            c = (u % 4) * 2 + i
            part = jnp.dot(ctxp[q, h], wv[c], preferred_element_type=F32)

            @pl.when(c == res_chunk)
            def _():
                finish(i, c, part + res[q, h].astype(F32) + bias[...])

            @pl.when(c != res_chunk)
            def _():
                finish(i, c, part)

    def p1(u):
        slot = u % 2

        @pl.when(u < 4)
        def _():
            for i in range(2):
                wv_load(u * 2 + i).wait()

        @pl.when(u >= 2)
        def _():
            wait_for(xsend.at[slot], xsend_sem.at[slot])

        def finish(i, c, part):
            xsend[slot, i] = part.astype(BF16).reshape(8, SUB, CW)

        product(1 - s, u, finish)
        h, chunks = pair_of(u)
        send(xsend.at[slot], xbuf.at[chunks, h], xsend_sem.at[slot], xrecv_sem.at[u], other_core)

    def p2(u):
        h, chunks = pair_of(u)
        wait_for(xbuf.at[chunks, h], xrecv_sem.at[u])

        def finish(i, c, part):
            total = part.reshape(8, SUB, CW) + xbuf[c, h].astype(F32)
            pbuf[c, h] = total.astype(BF16)

        product(s, u, finish)
        send(pbuf.at[chunks, h, far(2)], s1r.at[u], p_send, s1r_sem.at[u], xr)
        send(pbuf.at[chunks, h, own(2)], s1l.at[u], p_send, s1l_sem.at[u], xl)
        send(pbuf.at[chunks, h, own(1)], finl.at[u, 0], p_send, finl_sem.at[u, 0], xr)
        send(pbuf.at[chunks, h, far(3)], finr.at[u, 1], p_send, finr_sem.at[u, 1], xl)

    def p3(u):
        h, chunks = pair_of(u)
        wait_for(s1r.at[u], s1r_sem.at[u])
        piece = far(1)
        pbuf[chunks, h, piece] = (pbuf[chunks, h, piece].astype(F32) + s1r[u].astype(F32)).astype(BF16)
        send(pbuf.at[chunks, h, piece], finl.at[u, 1], p_send, finl_sem.at[u, 1], xr)
        wait_for(s1l.at[u], s1l_sem.at[u])
        piece = own(3)
        pbuf[chunks, h, piece] = (pbuf[chunks, h, piece].astype(F32) + s1l[u].astype(F32)).astype(BF16)
        send(pbuf.at[chunks, h, piece], finr.at[u, 0], p_send, finr_sem.at[u, 0], xl)

    def p4(u):
        h, chunks = pair_of(u)
        wait_for(finl.at[u, 1], finl_sem.at[u, 1])
        wait_for(finr.at[u, 1], finr_sem.at[u, 1])
        piece = far(0)
        pbuf[chunks, h, piece] = (
            pbuf[chunks, h, piece].astype(F32) + finl[u, 1].astype(F32) + finr[u, 1].astype(F32)
        ).astype(BF16)
        send(pbuf.at[chunks, h, piece], ybuf.at[u], p_send, y_sem.at[u], ypart)

    def p5(u):
        h, chunks = pair_of(u)
        wait_for(finl.at[u, 0], finl_sem.at[u, 0])
        wait_for(finr.at[u, 0], finr_sem.at[u, 0])
        wait_for(ybuf.at[u], y_sem.at[u])
        total = (
            pbuf[chunks, h, own(0)].astype(F32)
            + finl[u, 0].astype(F32)
            + finr[u, 0].astype(F32)
            + ybuf[u].astype(F32)
        )
        handoff = total.astype(BF16)
        hbuf[h, chunks] = handoff
        rowsum[h] += jnp.sum(jnp.sum(handoff.astype(F32), axis=0), axis=-1, keepdims=True)

    def gather1(piece, ssem, sem):
        mine = piece(own(0))
        send(mine, mine, ssem, sem(1), xr)
        send(mine, mine, ssem, sem(2), xl)
        send(mine, mine, ssem, sem(0), ypart)

    def gather2(piece, half, ssem, sem, xfirst):
        def pass_on(ref, index, to):
            send(ref, ref, ssem, sem(index), to)

        @pl.when(xfirst == 1)
        def _():
            wait_for(piece(own(3)), sem(1))
            pass_on(half(own(3), 0), 5, xr)
            pass_on(piece(own(3)), 3, ypart)
            wait_for(piece(own(1)), sem(2))
            pass_on(half(own(1), 1), 6, xl)
            pass_on(piece(own(1)), 4, ypart)

        @pl.when(xfirst == 0)
        def _():
            wait_for(piece(own(3)), sem(1))
            pass_on(piece(own(3)), 5, xr)
            wait_for(piece(far(0)), sem(0))
            pass_on(piece(far(0)), 4, xl)
            pass_on(piece(far(0)), 3, xr)

    def gather3(piece, half, ssem, sem, xfirst):
        def pass_on(ref, index, to):
            send(ref, ref, ssem, sem(index), to)

        @pl.when(xfirst == 1)
        def _():
            wait_for(half(own(2), 0), sem(5))
            wait_for(half(own(2), 1), sem(6))
            pass_on(piece(own(2)), 7, ypart)

        @pl.when(xfirst == 0)
        def _():
            wait_for(piece(far(1)), sem(4))
            pass_on(piece(far(1)), 6, xl)

    def gather4(piece, sem, xfirst):
        @pl.when(xfirst == 1)
        def _():
            wait_for(piece(far(0)), sem(0))
            wait_for(piece(far(3)), sem(3))
            wait_for(piece(far(1)), sem(4))
            wait_for(piece(far(2)), sem(7))

        @pl.when(xfirst == 0)
        def _():
            wait_for(piece(own(1)), sem(2))
            wait_for(piece(far(3)), sem(3))
            wait_for(piece(own(2)), sem(5))
            wait_for(piece(far(2)), sem(6))

    def order(j):
        step, mine = digit(RING_STEPS, j), digit(OWN_HALF, j)
        half = (yl + 1 + mine) % 2
        return half * 4 + (z + step) % 4, step, mine

    def g_refs(j):
        c = order(j)[0]

        def piece(device):
            return gbuf.at[c, pl.ds(s * SEQ_ROWS + device * PIECE, PIECE)]

        def half(device, i):
            return gbuf.at[c, pl.ds(s * SEQ_ROWS + device * PIECE + i * SUB, SUB)]

        def sem(i):
            return g_sem.at[j, i]

        return piece, half, sem

    def g1(j):
        piece, half, sem = g_refs(j)
        gather1(piece, g_send, sem)

    def g2(j):
        piece, half, sem = g_refs(j)
        gather2(piece, half, g_send, sem, digit(G_XFIRST, j))

    def g3(j):
        piece, half, sem = g_refs(j)
        gather3(piece, half, g_send, sem, digit(G_XFIRST, j))

    def g4(j):
        piece, half, sem = g_refs(j)
        gather4(piece, sem, digit(G_XFIRST, j))
        rows = pl.ds(s * SEQ_ROWS, SEQ_ROWS)
        c = order(j)[0]
        send(gbuf.at[c, rows], gbuf.at[c, rows], gc_send, gc_sem.at[j], other_core)

    def compute(j):
        c, step, mine = order(j)
        rows = pl.ds((1 - s) * SEQ_ROWS, SEQ_ROWS)
        wait_for(gbuf.at[c, rows], gc_sem.at[j])
        slot = j % 6

        @pl.when(j >= 6)
        def _():
            wait_for(wbuf.at[slot], ws1_send.at[slot])

        term = jnp.dot(ctxt[...], gbuf[c], preferred_element_type=F32).astype(BF16)
        wbuf[slot, 0] = term[:HALF]
        wbuf[slot, 1] = term[HALF:]

        @pl.when(j < 2)
        def _():
            send(wbuf.at[slot, 0], ws1r.at[mine], ws1_send.at[slot], ws1r_sem.at[mine], zr)
            send(wbuf.at[slot, 1], ws1l.at[mine], ws1_send.at[slot], ws1l_sem.at[mine], zl)

        @pl.when(step == 1)
        def _():
            send(wbuf.at[slot, 1], wfinl.at[mine, 1], w_send, wfinl_sem.at[mine, 1], zr)

        @pl.when(step == 3)
        def _():
            send(wbuf.at[slot, 0], wfinr.at[mine, 0], w_send, wfinr_sem.at[mine, 0], zl)

        back = gacc[...] + lax.dot_general(
            gbuf[c], wv[c], (((1,), (1,)), ((), ())), preferred_element_type=F32
        )

        @pl.when(j < CHUNKS - 1)
        def _():
            gacc[...] = back

        @pl.when(j == CHUNKS - 1)
        def _():
            gctx[...] = back.astype(BF16)
            pltpu.make_async_copy(gctx, gctx_hbm, out_sem.at[0]).start()

    def w2(j):
        _, step, mine = order(j)
        slot = j % 6

        @pl.when(step == 1)
        def _():
            wait_for(ws1r.at[mine], ws1r_sem.at[mine])
            wbuf[slot, 0] = (wbuf[slot, 0].astype(F32) + ws1r[mine].astype(F32)).astype(BF16)
            send(wbuf.at[slot, 0], wfinl.at[mine, 0], w_send, wfinl_sem.at[mine, 0], zr)

        @pl.when(step == 3)
        def _():
            wait_for(ws1l.at[mine], ws1l_sem.at[mine])
            wbuf[slot, 1] = (wbuf[slot, 1].astype(F32) + ws1l[mine].astype(F32)).astype(BF16)
            send(wbuf.at[slot, 1], wfinr.at[mine, 1], w_send, wfinr_sem.at[mine, 1], zl)

    def w3(_):
        for half in range(2):
            wait_for(wfinl.at[0, half], wfinl_sem.at[0, half])
            wait_for(wfinr.at[0, half], wfinr_sem.at[0, half])
            wbuf[4, half] = (
                wbuf[4, half].astype(F32) + wfinl[0, half].astype(F32) + wfinr[0, half].astype(F32)
            ).astype(BF16)
            send(wbuf.at[4, half], wy.at[half], wy_send.at[half], wy_sem.at[half], pair)

    def n_refs(u):
        h, chunks = pair_of(u)

        def piece(device):
            return xbuf.at[chunks, h, device]

        def half(device, i):
            return xbuf.at[(u % 4) * 2 + i, h, device]

        def sem(i):
            return n_sem.at[u, i]

        return piece, half, sem

    def norm(h):
        mean = rowsum[h] * (1.0 / WIDTH)

        def square(c, total):
            centred = hbuf[h, c].astype(F32) - mean
            return total + jnp.sum(centred * centred, axis=-1, keepdims=True)

        total = lax.fori_loop(0, CHUNKS, square, jnp.zeros((SUB, 1), F32))
        scale = lax.rsqrt(total * (1.0 / WIDTH) + EPSILON)

        for i in range(4):
            for c in (2 * i, 2 * i + 1):
                centred = hbuf[h, c].astype(F32) - mean
                cols = slice(c * CW, (c + 1) * CW)
                normed = centred * scale * gain[cols].reshape(1, CW) + nbias[cols].reshape(1, CW)
                xbuf[c, h, own(0)] = normed.astype(BF16)
            piece, half, sem = n_refs(h * 4 + i)
            gather1(piece, n_send, sem)

    def n2(u):
        piece, half, sem = n_refs(u)
        gather2(piece, half, n_send, sem, digit(N_XFIRST, u))

    def n3(u):
        piece, half, sem = n_refs(u)
        gather3(piece, half, n_send, sem, digit(N_XFIRST, u))

    def q(u):
        piece, half, sem = n_refs(u)
        gather4(piece, sem, digit(N_XFIRST, u))
        h = u // 4
        wq_load(u).wait()
        slot = u % WQ_SLOTS
        total = qacc[h]
        for i in range(2):
            rows = xbuf[(u % 4) * 2 + i, h].reshape(8 * SUB, CW)
            total += jnp.dot(rows, wq[slot, i * CW:(i + 1) * CW], preferred_element_type=F32)

        @pl.when(u % 4 < 3)
        def _():
            qacc[h] = total

        @pl.when(u % 4 == 3)
        def _():
            full = total + qbias[...].reshape(1, QCOLS)
            query[h] = full.astype(BF16).reshape(8, SUB, QCOLS)
            pltpu.make_async_copy(query.at[h], query_hbm.at[:, h], out_sem.at[2 + h]).start()

        @pl.when(u + WQ_SLOTS < UNITS)
        def _():
            wq_load(u + WQ_SLOTS).start()

    bodies = {
        "g1": g1, "p1": p1, "p2": p2, "p3": p3, "p4": p4, "p5": p5, "g2": g2, "g3": g3, "g4": g4,
        "c": compute, "w2": w2, "w3": w3, "norm": norm, "n2": n2, "n3": n3, "q": q,
    }

    def mask(name, span):
        return sum(1 << (k - span * SPAN) for k in SCHEDULE[name] if k // SPAN == span)

    def tick(k, state):
        later = []
        for i, name in enumerate(SCHEDULE):
            left, index = state[2 * i], state[2 * i + 1]
            active = left % 2

            @pl.when(active == 1)
            def _():
                bodies[name](index)

            left = left // 2
            for span in range(1, spans):
                if mask(name, span):
                    left = left + mask(name, span) * ((k + 1) // (span * SPAN) - k // (span * SPAN))
            later += [left, index + active]
        return tuple(later)

    ticks = 1 + max(max(v) for v in SCHEDULE.values())
    spans = (ticks + SPAN - 1) // SPAN
    start = []
    for name in SCHEDULE:
        start += [jnp.int32(mask(name, 0)), jnp.int32(0)]
    lax.fori_loop(0, ticks, tick, tuple(start))

    for half in range(2):
        wait_for(wfinl.at[1, half], wfinl_sem.at[1, half])
        wait_for(wfinr.at[1, half], wfinr_sem.at[1, half])
        wait_for(wy.at[half], wy_sem.at[half])
        wbuf[1, half] = (
            wbuf[1, half].astype(F32)
            + wfinl[1, half].astype(F32)
            + wfinr[1, half].astype(F32)
            + wy[half].astype(F32)
        ).astype(BF16)
    pltpu.make_async_copy(wbuf.at[1], gow_hbm, out_sem.at[1]).start()

    pltpu.make_async_copy(gctx, gctx_hbm, out_sem.at[0]).wait()
    for h in range(2):
        pltpu.make_async_copy(query.at[h], query_hbm.at[:, h], out_sem.at[2 + h]).wait()
    pltpu.make_async_copy(wbuf.at[1], gow_hbm, out_sem.at[1]).wait()

    for slot in range(2):
        wait_for(xsend.at[slot], xsend_sem.at[slot])
        wait_for(wy.at[slot], wy_send.at[slot])
    wait_for(pbuf.at[:, :, pl.ds(0, 7)], p_send)
    wait_for(gbuf.at[:, pl.ds(0, 224)], g_send)
    wait_for(gbuf.at[:, pl.ds(0, 256)], gc_send)
    wait_for(xbuf.at[:, :, pl.ds(0, 7)], n_send)
    wait_for(wbuf.at[pl.ds(2, 4)], w_send)


def store(*refs):
    sources, results, sems = refs[:3], refs[3:6], refs[6]
    copies = [pltpu.make_async_copy(a, b, sems.at[i]) for i, (a, b) in enumerate(zip(sources, results))]
    for copy in copies:
        copy.start()
    for copy in copies:
        copy.wait()


def local(
    context, residual, out_weight, out_bias, norm_gain, norm_bias, query_weight, query_bias, grad_handoff
):
    rows = 2 * SEQ_ROWS
    yh = lax.axis_index("tensor") % 2
    zero = jnp.zeros_like(out_bias)
    wide_bias = jnp.where(
        yh == 0, jnp.concatenate([out_bias, zero]), jnp.concatenate([zero, out_bias])
    ).reshape(1, CW)

    dma = pltpu.SemaphoreType.DMA
    any_spec = pl.BlockSpec(memory_space=pl.ANY)
    results = (
        jax.ShapeDtypeStruct((8, 2, SUB, QCOLS), BF16),
        jax.ShapeDtypeStruct((rows, HEADS), BF16),
        jax.ShapeDtypeStruct((2, HALF, CW), BF16),
    )
    parts = pl.pallas_call(
        kernel,
        out_shape=results,
        in_specs=[any_spec] * 9,
        out_specs=(any_spec,) * 3,
        scratch_shapes=[
            pltpu.VMEM((rows, HEADS), BF16),
            pltpu.VMEM((2, 2, 8 * SUB, HEADS), BF16),
            pltpu.VMEM((HEADS, rows), BF16),
            pltpu.VMEM((2, CW, SEQ_ROWS), BF16),
            pltpu.VMEM((2, 2, 8 * SUB, CW), BF16),
            pltpu.VMEM((1, CW), F32),
            pltpu.VMEM((WIDTH,), F32),
            pltpu.VMEM((WIDTH,), F32),
            pltpu.VMEM((QCOLS,), F32),
            pltpu.VMEM((CHUNKS, HEADS, CW), BF16),
            pltpu.VMEM((2, 2, 8, SUB, CW), BF16),
            pltpu.VMEM((CHUNKS, 2, 8, SUB, CW), BF16),
            pltpu.VMEM((CHUNKS, 2, 8, SUB, CW), BF16),
            pltpu.VMEM((UNITS, 2, SUB, CW), BF16),
            pltpu.VMEM((UNITS, 2, SUB, CW), BF16),
            pltpu.VMEM((UNITS, 2, 2, SUB, CW), BF16),
            pltpu.VMEM((UNITS, 2, 2, SUB, CW), BF16),
            pltpu.VMEM((UNITS, 2, SUB, CW), BF16),
            pltpu.VMEM((2, CHUNKS, SUB, CW), BF16),
            pltpu.VMEM((WQ_SLOTS, 2 * CW, QCOLS), BF16),
            pltpu.VMEM((CHUNKS, rows, CW), BF16),
            pltpu.VMEM((6, 2, HALF, CW), BF16),
            pltpu.VMEM((2, HALF, CW), BF16),
            pltpu.VMEM((2, HALF, CW), BF16),
            pltpu.VMEM((2, 2, HALF, CW), BF16),
            pltpu.VMEM((2, 2, HALF, CW), BF16),
            pltpu.VMEM((2, HALF, CW), BF16),
            pltpu.VMEM((rows, HEADS), F32),
            pltpu.VMEM((2, 8 * SUB, QCOLS), F32),
            pltpu.VMEM((2, SUB, 1), F32),
            pltpu.VMEM((rows, HEADS), BF16),
            pltpu.VMEM((2, 8, SUB, QCOLS), BF16),
            dma((7,)),
            dma((CHUNKS,)),
            dma((WQ_SLOTS,)),
            dma((CHUNKS,)),
            dma((4,)),
            dma((2,)),
            dma((UNITS,)),
            dma,
            dma((UNITS,)),
            dma((UNITS,)),
            dma((UNITS, 2)),
            dma((UNITS, 2)),
            dma((UNITS,)),
            dma,
            dma,
            dma((CHUNKS, 8)),
            dma((CHUNKS,)),
            dma,
            dma((UNITS, 8)),
            dma,
            dma((2,)),
            dma((2,)),
            dma((2,)),
            dma((2, 2)),
            dma((2, 2)),
            dma((2,)),
            dma((2,)),
        ],
        compiler_params=pltpu.CompilerParams(
            collective_id=0, has_side_effects=True, vmem_limit_bytes=62 * 2**20
        ),
    )(
        context.reshape(rows, HEADS),
        residual.transpose(0, 2, 1),
        out_weight,
        wide_bias,
        norm_gain,
        norm_bias,
        query_weight,
        query_bias,
        grad_handoff.reshape(PIECE, WIDTH),
    )
    query, gctx, gow = pl.pallas_call(
        store,
        out_shape=results,
        in_specs=[pl.BlockSpec(memory_space=pltpu.VMEM)] * 3,
        out_specs=(any_spec,) * 3,
        scratch_shapes=[dma((3,))],
    )(*parts)
    return (
        query.reshape(1, SEQ_ROWS, QCOLS),
        gctx.reshape(2, SEQ_ROWS, HEADS),
        gow.reshape(HEADS, CW),
    )


def solution(mesh):
    in_specs = (
        P(None, "dp", ("section", "tensor")),
        P(None, "dp", ("section", "tensor")),
        P(("section", "tensor"), None),
        P(("section", "tensor")),
        P(),
        P(),
        P(None, "tensor"),
        P("tensor"),
        P("section", ("dp", "tensor"), None),
    )
    out_specs = (
        P("section", "dp", "tensor"),
        P(None, "dp", ("section", "tensor")),
        P(("section", "tensor"), "dp"),
    )
    return jax.shard_map(local, mesh=mesh, in_specs=in_specs, out_specs=out_specs, check_vma=False)
```

time: 387 us -> 112 us (0.29)
  waiting for transfers between devices: 307 us -> 0 us
  Pallas kernels: 0 us -> 110 us
  matrix products: 43.8 us -> 0 us
  between operations: 13.8 us -> 0.65 us
  local copies, waits for them, and re-layouts: 13.4 us -> 0.6 us
  other arithmetic: 8.8 us -> 0.84 us
    all_gather x2 -> x0, waiting for transfers between devices: 148 us -> none  [the longest x1 76.3 us: local(): lax.all_gather(handoff, ('section', 'tensor'), axis=2, tiled=True)]
    pallas_call x0 -> x2, Pallas kernels: none -> 110 us  [the longest x1 107 us: local(): pl.pallas_call(kernel, out_shape=results, in_specs=[any_spec] * 9, out_sp...]
    reduce_scatter x1 -> x0, waiting for transfers between devices: 87.5 us -> none  [local(): lax.psum_scatter(partial_value.astype(jnp.bfloat16), ('section', 'tensor'...]
    unnamed x5 -> x0, waiting for transfers between devices: 71.3 us -> none
    dot_general x4 -> x0, matrix products: 43.8 us -> none  [the longest x1 12.5 us: local(): jnp.dot(normed.reshape(row_count, width), query_weight, preferred_element...]
    unnamed x18 -> x0, local copies, waits for them, and re-layouts: 13.4 us -> none
    reduce_sum x2 -> x0, other arithmetic: 6.71 us -> none  [the longest x1 3.57 us: layer_norm(): variance = jnp.mean(centred * centred, axis=-1, keepdims=True)]
  transfers between devices with their start and end apart: 4 -> 0, of which waited for: 4 -> 0; matrix products, arithmetic and copies ran while one was open for 12% -> 0% of each run, Pallas kernels for 0% -> 0%
where the time goes in v2:
time: 112 us
  Pallas kernels  110 us (98%)
    pallas_call x1, Pallas kernels, local(): pl.pallas_call(kernel, out_shape=results, in_specs=[any_spec] * 9, out_sp...  107 us
    pallas_call x1, Pallas kernels, local(): pl.pallas_call(store, out_shape=results, in_specs=[pl.BlockSpec(memory_sp...  2.61 us

profile of v2, /device:TPU:1, one launch (start us, length us, event | category | flops | bytes accessed | tf_op | source)
XLA Modules:
  0.0 111.9 jit_solution(16872584599746077997)
XLA Ops:
  0.6 0.8 pad_select_fusion
  1.5 0.6 reshape.25.bias_hbm
  2.1 107.2 %shard_map.112 = (bf16[8,2,16,768]{3,2,1,0:T(8,128)(2,1)}, bf16[512,384]{1,0:T(8,128)(2,1)}, bf16[2,192,1152]{2,1,0:T(8,128)(2,1)}) custom-call(bf16[512,384]{1,0:T(8,128)(2,1)} %bitcast.8, bf16[2,576,256]{2,1,0:T(8,128)(2,1)} %bitcast.6, bf16[384,9216]{1,0:T(8,128)(2,1)} %ow_hbm.1, f32[1,1152]{1,0:T(1,128)} %reshape.25.bias_hbm, f32[9216]{0:T(1024)} %gain_hbm.1, ...), custom_call_target="tpu_custom_call" | custom-call | tf_op jit(solution)/shard_map/pallas_call | solution.py:570
  109.3 2.6 %shard_map.113 = (bf16[8,2,16,768]{3,2,1,0:T(8,128)(2,1)}, bf16[512,384]{1,0:T(8,128)(2,1)}, bf16[2,192,1152]{2,1,0:T(8,128)(2,1)}) custom-call(bf16[8,2,16,768]{3,2,1,0:T(8,128)(2,1)} %get-tuple-element.9.refs_0_, bf16[512,384]{1,0:T(8,128)(2,1)} %get-tuple-element.10.refs_1_, bf16[2,192,1152]{2,1,0:T(8,128)(2,1)} %get-tuple-element.11.refs_2_), custom_call_target="tpu_custom_call" | custom-call | tf_op jit(solution)/shard_map/pallas_call | solution.py:650

commit v3 on v2

v3 whole, which is shorter than its diff:
```python
import jax
import jax.numpy as jnp
from jax import lax
from jax.experimental import pallas as pl
from jax.experimental.pallas import tpu as pltpu
from jax.sharding import PartitionSpec as P

EPSILON = 1e-05
MESH = pl.DeviceIdType.MESH
BF16 = jnp.bfloat16
F32 = jnp.float32

CHUNKS = 8
CW = 1152
WIDTH = CHUNKS * CW
FEATS = WIDTH // 16
SEQ_ROWS = 256
PIECE = 32
SUB = 16
UNITS = 8
HEADS = 384
HALF = HEADS // 2
QCOLS = 768
WQ_SLOTS = 2

SCHEDULE = {
    "w3": (44,),
    "g1": (0, 1, 2, 3, 4, 5, 7, 29),
    "prep": (3,),
    "prep2": (12,),
    "n2": (36, 37, 38, 39, 44, 45, 46, 47),
    "p2": (7, 8, 11, 13, 15, 17, 18, 22),
    "g2": (7, 9, 11, 12, 14, 18, 22, 38),
    "p1": (4, 5, 6, 7, 8, 9, 10, 11),
    "g4": (16, 18, 20, 22, 27, 31, 35, 46),
    "w2": (19, 25, 27, 28, 30, 35, 36, 50),
    "p5": (22, 23, 26, 32, 35, 39, 40, 41),
    "p4": (15, 16, 18, 28, 32, 33, 34, 35),
    "norm": (32, 41),
    "n3": (39, 40, 41, 42, 48, 49, 50, 51),
    "g3": (12, 13, 14, 15, 20, 26, 31, 41),
    "q": (42, 43, 45, 47, 51, 52, 53, 54),
    "p3": (11, 12, 13, 18, 23, 24, 25, 29),
    "w4": (50, 54),
    "c": (17, 20, 21, 25, 28, 32, 35, 47),
}
G_XFIRST = (1, 1, 1, 1, 1, 1, 1, 0)
N_XFIRST = (1, 0, 0, 0, 0, 0, 0, 0)
SPAN = 30

RING_STEPS = (2, 2, 1, 3, 0, 1, 3, 0)
OWN_HALF = (0, 1, 0, 0, 0, 1, 1, 1)


def digit(table, j):
    packed = sum(v * 4**i for i, v in enumerate(table))
    scale = (1 + 3 * (j % 2)) * (1 + 15 * ((j // 2) % 2)) * (1 + 255 * (j // 4))
    return (packed // scale) % 4


def wait_for(ref, sem):
    pltpu.make_async_copy(ref, ref, sem).wait()


def kernel(
    ctx_hbm, res_hbm, ow_hbm, bias_hbm, gain_hbm, nbias_hbm, qw_hbm, qbias_hbm, grad_hbm,
    query_ref, gctx_ref, gow_ref,
    ctx, ctxp, ctxt, rest, res, bias, wide, gain, nbias, qbias, wv, xsend, xbuf, pbuf,
    s1, fin, hbuf,
    wq, gbuf, wbuf, ws1r, ws1l, wfin, gacc, qacc, rowsum,
    in_sem, wv_sem, wq_sem, gin_sem,
    xsend_sem, xrecv_sem, p_send, s1_sem, fin_sem,
    g_send, gc_send, g_sem, gc_sem, n_send, n_sem,
    w_send, ws1_send, ws1r_sem, ws1l_sem, wfin_sem, wy_send,
):
    s = lax.axis_index("section")
    d = lax.axis_index("dp")
    t = lax.axis_index("tensor")
    x, yh = t // 2, t % 2
    yl, z = d // 4, d % 4
    other_core = (1 - s, d, t)
    xr = (s, d, ((x + 1) % 4) * 2 + yh)
    xl = (s, d, ((x + 3) % 4) * 2 + yh)
    ypart = (s, d, x * 2 + (1 - yh))
    zr = (s, yl * 4 + (z + 1) % 4, t)
    zl = (s, yl * 4 + (z + 3) % 4, t)
    pair = (s, (1 - yl) * 4 + z, t)

    def send(src, dst, ssem, rsem, to):
        pltpu.make_async_remote_copy(
            src_ref=src, dst_ref=dst, send_sem=ssem, recv_sem=rsem, device_id=to, device_id_type=MESH
        ).start()

    def own(offset):
        return ((x + offset) % 4) * 2 + yh

    def far(offset):
        return ((x + offset) % 4) * 2 + 1 - yh

    barrier = pltpu.get_barrier_semaphore()
    neighbours = (other_core, xr, xl, ypart, zr, zl, pair)
    for to in neighbours:
        pl.semaphore_signal(barrier, inc=1, device_id=to, device_id_type=MESH)

    small = [
        pltpu.make_async_copy(ctx_hbm, ctx, in_sem.at[0]),
        pltpu.make_async_copy(gain_hbm, gain, in_sem.at[1]),
        pltpu.make_async_copy(nbias_hbm, nbias, in_sem.at[2]),
        pltpu.make_async_copy(qbias_hbm, qbias, in_sem.at[3]),
        pltpu.make_async_copy(bias_hbm, bias, in_sem.at[4]),
    ] + [
        pltpu.make_async_copy(
            res_hbm.at[q],
            rest.at[q, pl.ds(pl.multiple_of(yh * FEATS, 16), FEATS)],
            in_sem.at[5 + q],
        )
        for q in range(2)
    ]
    for load in small:
        load.start()

    def wv_load(c):
        return pltpu.make_async_copy(
            ow_hbm.at[:, pl.ds(pl.multiple_of(c * CW, 128), CW)], wv.at[c], wv_sem.at[c // 2]
        )

    def gin_load(c):
        return pltpu.make_async_copy(
            grad_hbm.at[:, pl.ds(pl.multiple_of(c * CW, 128), CW)],
            gbuf.at[c, pl.ds(s * SEQ_ROWS + t * PIECE, PIECE)],
            gin_sem,
        )

    def wq_load(c):
        return pltpu.make_async_copy(
            qw_hbm.at[pl.ds((c % 4) * 2 * CW, 2 * CW)], wq.at[c % WQ_SLOTS], wq_sem.at[c % WQ_SLOTS]
        )

    @pl.loop(0, CHUNKS)
    def _(c):
        gin_load(c).start()

    wv_load(0).start()

    @pl.loop(1, CHUNKS)
    def _(c):
        wv_load(c).start()

    @pl.loop(0, WQ_SLOTS)
    def _(c):
        wq_load(c).start()

    wait_for(gbuf.at[:, pl.ds(0, PIECE)], gin_sem)
    pl.semaphore_wait(barrier, len(neighbours))

    def prep(_):
        for load in small:
            load.wait()
        edge = bias[...].reshape(1, FEATS)
        blank = jnp.zeros_like(edge)

        @pl.when(yh == 0)
        def _():
            wide[...] = jnp.concatenate([edge, blank], axis=1)

        @pl.when(yh == 1)
        def _():
            wide[...] = jnp.concatenate([blank, edge], axis=1)

        for q in range(2):
            rest[q, pl.ds(pl.multiple_of((1 - yh) * FEATS, 16), FEATS)] = jnp.zeros(
                (FEATS, SEQ_ROWS), BF16
            )
            by_row = rest[q].T
            for t_ in range(8):
                for h in range(2):
                    rows = slice(t_ * PIECE + h * SUB, t_ * PIECE + (h + 1) * SUB)
                    ctxp[q, h, t_ * SUB:(t_ + 1) * SUB] = ctx[
                        q * SEQ_ROWS + rows.start:q * SEQ_ROWS + rows.stop
                    ]
                    res[q, h, t_ * SUB:(t_ + 1) * SUB] = by_row[rows]

    def prep2(_):
        gacc[...] = jnp.zeros_like(gacc)
        qacc[...] = jnp.zeros_like(qacc)
        rowsum[...] = jnp.zeros_like(rowsum)
        ctxt[...] = ctx[...].T

    res_chunk = 4 * s + x

    def pair_of(u):
        return u // 4, pl.ds((u % 4) * 2, 2)

    def product(q, u, finish):
        h = u // 4
        for i in range(2):
            c = (u % 4) * 2 + i
            part = jnp.dot(ctxp[q, h], wv[c], preferred_element_type=F32)

            @pl.when(c == res_chunk)
            def _():
                finish(i, c, part + res[q, h].astype(F32) + wide[...])

            @pl.when(c != res_chunk)
            def _():
                finish(i, c, part)

    def p1(u):
        slot = u % 2

        @pl.when(u < 4)
        def _():
            wait_for(wv.at[pair_of(u)[1]], wv_sem.at[u])

        @pl.when(u >= 2)
        def _():
            wait_for(xsend.at[slot], xsend_sem.at[slot])

        def finish(i, c, part):
            xsend[slot, i] = part.astype(BF16).reshape(8, SUB, CW)

        product(1 - s, u, finish)
        h, chunks = pair_of(u)
        send(xsend.at[slot], xbuf.at[chunks, h], xsend_sem.at[slot], xrecv_sem.at[u], other_core)

    def p2(u):
        h, chunks = pair_of(u)
        wait_for(xbuf.at[chunks, h], xrecv_sem.at[u])

        def finish(i, c, part):
            total = part.reshape(8, SUB, CW) + xbuf[c, h].astype(F32)
            pbuf[c, h] = total.astype(BF16)

        product(s, u, finish)
        send(pbuf.at[chunks, h, far(2)], s1.at[u, 0], p_send, s1_sem.at[u], xr)
        send(pbuf.at[chunks, h, own(2)], s1.at[u, 1], p_send, s1_sem.at[u], xl)
        send(pbuf.at[chunks, h, own(1)], fin.at[u, 0, 0], p_send, fin_sem.at[u, 0], xr)
        send(pbuf.at[chunks, h, far(3)], fin.at[u, 1, 1], p_send, fin_sem.at[u, 1], xl)

    def p3(u):
        h, chunks = pair_of(u)
        wait_for(s1.at[u], s1_sem.at[u])
        piece = far(1)
        pbuf[chunks, h, piece] = (pbuf[chunks, h, piece].astype(F32) + s1[u, 0].astype(F32)).astype(BF16)
        send(pbuf.at[chunks, h, piece], fin.at[u, 1, 0], p_send, fin_sem.at[u, 1], xr)
        piece = own(3)
        pbuf[chunks, h, piece] = (pbuf[chunks, h, piece].astype(F32) + s1[u, 1].astype(F32)).astype(BF16)
        send(pbuf.at[chunks, h, piece], fin.at[u, 0, 1], p_send, fin_sem.at[u, 0], xl)

    def p4(u):
        h, chunks = pair_of(u)
        wait_for(fin.at[u, 1, pl.ds(0, 2)], fin_sem.at[u, 1])
        piece = far(0)
        pbuf[chunks, h, piece] = (
            pbuf[chunks, h, piece].astype(F32) + fin[u, 1, 0].astype(F32) + fin[u, 1, 1].astype(F32)
        ).astype(BF16)
        send(pbuf.at[chunks, h, piece], fin.at[u, 0, 2], p_send, fin_sem.at[u, 0], ypart)

    def p5(u):
        h, chunks = pair_of(u)
        wait_for(fin.at[u, 0], fin_sem.at[u, 0])
        total = (
            pbuf[chunks, h, own(0)].astype(F32)
            + fin[u, 0, 0].astype(F32)
            + fin[u, 0, 1].astype(F32)
            + fin[u, 0, 2].astype(F32)
        )
        handoff = total.astype(BF16)
        hbuf[h, chunks] = handoff
        rowsum[h] += jnp.sum(jnp.sum(handoff.astype(F32), axis=0), axis=-1, keepdims=True)

    def gather1(piece, ssem, sem, xfirst, ydev):
        mine = piece(own(0))
        send(mine, mine, ssem, sem(0), xr)
        send(mine, mine, ssem, sem(3 - 2 * xfirst), xl)
        send(mine, mine, ssem, sem(1 + 2 * xfirst), ydev)

    def gather2(piece, half, ssem, sem, xfirst, ydev):
        def pass_on(ref, index, to):
            send(ref, ref, ssem, sem(index), to)

        @pl.when(xfirst == 1)
        def _():
            wait_for(piece(own(3)), sem(0))
            pass_on(half(own(3), 0), 2, xr)
            pass_on(piece(own(3)), 3, ydev)
            wait_for(piece(own(1)), sem(1))
            pass_on(half(own(1), 1), 2, xl)
            pass_on(piece(own(1)), 3, ydev)

        @pl.when(xfirst == 0)
        def _():
            wait_for(piece(own(3)), sem(0))
            pass_on(piece(own(3)), 3, xr)
            wait_for(piece(far(0)), sem(1))
            pass_on(piece(far(0)), 2, xl)
            pass_on(piece(far(0)), 3, xr)

    def gather3(piece, ssem, sem, xfirst, ydev):
        def pass_on(ref, index, to):
            send(ref, ref, ssem, sem(index), to)

        @pl.when(xfirst == 1)
        def _():
            wait_for(piece(own(2)), sem(2))
            pass_on(piece(own(2)), 3, ydev)

        @pl.when(xfirst == 0)
        def _():
            wait_for(piece(far(1)), sem(2))
            pass_on(piece(far(1)), 3, xl)

    def gather4(four, sem):
        wait_for(four, sem(3))

    def order(j):
        step, mine = digit(RING_STEPS, j), digit(OWN_HALF, j)
        half = (yl + 1 + mine) % 2
        return half * 4 + (z + step) % 4, step, mine

    def g_refs(j):
        c = order(j)[0]

        def piece(device):
            return gbuf.at[c, pl.ds(s * SEQ_ROWS + device * PIECE, PIECE)]

        def half(device, i):
            return gbuf.at[c, pl.ds(s * SEQ_ROWS + device * PIECE + i * SUB, SUB)]

        def sem(i):
            return g_sem.at[j, i]

        return piece, half, sem, digit(G_XFIRST, j)

    def g1(j):
        piece, half, sem, xfirst = g_refs(j)
        gather1(piece, g_send, sem, xfirst, ypart)

    def g2(j):
        piece, half, sem, xfirst = g_refs(j)
        gather2(piece, half, g_send, sem, xfirst, ypart)

    def g3(j):
        piece, half, sem, xfirst = g_refs(j)
        gather3(piece, g_send, sem, xfirst, ypart)

    def g4(j):
        piece, half, sem, xfirst = g_refs(j)
        c = order(j)[0]
        gather4(gbuf.at[c, pl.ds(0, 4 * PIECE)], sem)
        rows = pl.ds(s * SEQ_ROWS, SEQ_ROWS)
        send(gbuf.at[c, rows], gbuf.at[c, rows], gc_send, gc_sem.at[j], other_core)

    def compute(j):
        c, step, mine = order(j)
        rows = pl.ds((1 - s) * SEQ_ROWS, SEQ_ROWS)
        wait_for(gbuf.at[c, rows], gc_sem.at[j])
        slot = j % 6

        @pl.when(j >= 6)
        def _():
            wait_for(wbuf.at[slot], ws1_send.at[slot])

        term = jnp.dot(ctxt[...], gbuf[c], preferred_element_type=F32).astype(BF16)
        wbuf[slot, 0] = term[:HALF]
        wbuf[slot, 1] = term[HALF:]

        @pl.when(j < 2)
        def _():
            send(wbuf.at[slot, 0], ws1r.at[mine], ws1_send.at[slot], ws1r_sem.at[mine], zr)
            send(wbuf.at[slot, 1], ws1l.at[mine], ws1_send.at[slot], ws1l_sem.at[mine], zl)

        @pl.when(step == 1)
        def _():
            send(wbuf.at[slot, 1], wfin.at[mine, 1, 0], w_send, wfin_sem.at[mine, 1], zr)

        @pl.when(step == 3)
        def _():
            send(wbuf.at[slot, 0], wfin.at[mine, 0, 1], w_send, wfin_sem.at[mine, 0], zl)

        back = gacc[...] + lax.dot_general(
            gbuf[c], wv[c], (((1,), (1,)), ((), ())), preferred_element_type=F32
        )

        @pl.when(j < CHUNKS - 1)
        def _():
            gacc[...] = back

        @pl.when(j == CHUNKS - 1)
        def _():
            gctx_ref[...] = back.astype(BF16)

    def w2(j):
        _, step, mine = order(j)
        slot = j % 6

        @pl.when(step == 1)
        def _():
            wait_for(ws1r.at[mine], ws1r_sem.at[mine])
            wbuf[slot, 0] = (wbuf[slot, 0].astype(F32) + ws1r[mine].astype(F32)).astype(BF16)
            send(wbuf.at[slot, 0], wfin.at[mine, 0, 0], w_send, wfin_sem.at[mine, 0], zr)

        @pl.when(step == 3)
        def _():
            wait_for(ws1l.at[mine], ws1l_sem.at[mine])
            wbuf[slot, 1] = (wbuf[slot, 1].astype(F32) + ws1l[mine].astype(F32)).astype(BF16)
            send(wbuf.at[slot, 1], wfin.at[mine, 1, 1], w_send, wfin_sem.at[mine, 1], zl)

    def w3(_):
        for half in range(2):
            wait_for(wfin.at[0, half, pl.ds(0, 2)], wfin_sem.at[0, half])
            wbuf[4, half] = (
                wbuf[4, half].astype(F32) + wfin[0, half, 0].astype(F32) + wfin[0, half, 1].astype(F32)
            ).astype(BF16)
            send(wbuf.at[4, half], wfin.at[1, half, 2], wy_send.at[half], wfin_sem.at[1, half], pair)

    def w4(half):
        wait_for(wfin.at[1, half], wfin_sem.at[1, half])
        gow_ref[half] = (
            wbuf[1, half].astype(F32)
            + wfin[1, half, 0].astype(F32)
            + wfin[1, half, 1].astype(F32)
            + wfin[1, half, 2].astype(F32)
        ).astype(BF16)

    def n_refs(u):
        h, chunks = pair_of(u)

        def piece(device):
            return xbuf.at[chunks, h, device]

        def half(device, i):
            return xbuf.at[(u % 4) * 2 + i, h, device]

        def sem(i):
            return n_sem.at[u, i]

        return piece, half, sem, digit(N_XFIRST, u)

    def norm(h):
        mean = rowsum[h] * (1.0 / WIDTH)

        def square(c, total):
            centred = hbuf[h, c].astype(F32) - mean
            return total + jnp.sum(centred * centred, axis=-1, keepdims=True)

        total = lax.fori_loop(0, CHUNKS, square, jnp.zeros((SUB, 1), F32))
        scale = lax.rsqrt(total * (1.0 / WIDTH) + EPSILON)

        for i in range(4):
            for c in (2 * i, 2 * i + 1):
                centred = hbuf[h, c].astype(F32) - mean
                cols = slice(c * CW, (c + 1) * CW)
                normed = centred * scale * gain[cols].reshape(1, CW) + nbias[cols].reshape(1, CW)
                xbuf[c, h, own(0)] = normed.astype(BF16)
            piece, half, sem, xfirst = n_refs(h * 4 + i)
            gather1(piece, n_send, sem, xfirst, ypart)

    def n2(u):
        piece, half, sem, xfirst = n_refs(u)
        gather2(piece, half, n_send, sem, xfirst, ypart)

    def n3(u):
        piece, half, sem, xfirst = n_refs(u)
        gather3(piece, n_send, sem, xfirst, ypart)

    def q(u):
        piece, half, sem, xfirst = n_refs(u)
        chunks = pair_of(u)[1]
        gather4(xbuf.at[chunks, 0, pl.ds(0, 4)], sem)
        h = u // 4
        wq_load(u).wait()
        slot = u % WQ_SLOTS
        total = qacc[h]
        for i in range(2):
            rows = xbuf[(u % 4) * 2 + i, h].reshape(8 * SUB, CW)
            total += jnp.dot(rows, wq[slot, i * CW:(i + 1) * CW], preferred_element_type=F32)

        @pl.when(u % 4 < 3)
        def _():
            qacc[h] = total

        @pl.when(u % 4 == 3)
        def _():
            full = total + qbias[...].reshape(1, QCOLS)
            query_ref[:, h] = full.astype(BF16).reshape(8, SUB, QCOLS)

        @pl.when(u + WQ_SLOTS < UNITS)
        def _():
            wq_load(u + WQ_SLOTS).start()

    bodies = {
        "g1": g1, "p1": p1, "p2": p2, "p3": p3, "p4": p4, "p5": p5, "g2": g2, "g3": g3, "g4": g4,
        "c": compute, "w2": w2, "w3": w3, "w4": w4, "prep": prep, "prep2": prep2, "norm": norm, "n2": n2, "n3": n3, "q": q,
    }

    def mask(name, span):
        return sum(1 << (k - span * SPAN) for k in SCHEDULE[name] if k // SPAN == span)

    def tick(k, state):
        later = []
        for i, name in enumerate(SCHEDULE):
            left, index = state[2 * i], state[2 * i + 1]
            active = left % 2

            @pl.when(active == 1)
            def _():
                bodies[name](index)

            left = left // 2
            for span in range(1, spans):
                if mask(name, span):
                    turn = ((k + 1) // (span * SPAN) - k // (span * SPAN)) * (1 - k // (span * SPAN))
                    left = left + mask(name, span) * turn
            later += [left, index + active]
        return tuple(later)

    ticks = 1 + max(max(v) for v in SCHEDULE.values())
    spans = (ticks + SPAN - 1) // SPAN
    start = []
    for name in SCHEDULE:
        start += [jnp.int32(mask(name, 0)), jnp.int32(0)]
    lax.fori_loop(0, ticks, tick, tuple(start))

    for slot in range(2):
        wait_for(xsend.at[slot], xsend_sem.at[slot])
        wait_for(wbuf.at[4, slot], wy_send.at[slot])
    wait_for(pbuf.at[:, :, pl.ds(0, 7)], p_send)
    wait_for(gbuf.at[:, pl.ds(0, 224)], g_send)
    wait_for(gbuf.at[:, pl.ds(0, 256)], gc_send)
    wait_for(xbuf.at[:, :, pl.ds(0, 7)], n_send)
    wait_for(wbuf.at[pl.ds(2, 4)], w_send)


def store(*refs):
    sources, results, sems = refs[:3], refs[3:6], refs[6]
    copies = [pltpu.make_async_copy(a, b, sems.at[i]) for i, (a, b) in enumerate(zip(sources, results))]
    for copy in copies:
        copy.start()
    for copy in copies:
        copy.wait()


def local(
    context, residual, out_weight, out_bias, norm_gain, norm_bias, query_weight, query_bias, grad_handoff
):
    rows = 2 * SEQ_ROWS

    dma = pltpu.SemaphoreType.DMA
    any_spec = pl.BlockSpec(memory_space=pl.ANY)
    shapes = ((8, 2, SUB, QCOLS), (rows, HEADS), (2, HALF, CW))
    parts = pl.pallas_call(
        kernel,
        out_shape=tuple(pltpu.VMEM(shape, BF16) for shape in shapes),
        in_specs=[any_spec] * 9,
        out_specs=(pl.BlockSpec(memory_space=pltpu.VMEM),) * 3,
        scratch_shapes=[
            pltpu.VMEM((rows, HEADS), BF16),
            pltpu.VMEM((2, 2, 8 * SUB, HEADS), BF16),
            pltpu.VMEM((HEADS, rows), BF16),
            pltpu.VMEM((2, CW, SEQ_ROWS), BF16),
            pltpu.VMEM((2, 2, 8 * SUB, CW), BF16),
            pltpu.VMEM((FEATS,), F32),
            pltpu.VMEM((1, CW), F32),
            pltpu.VMEM((WIDTH,), F32),
            pltpu.VMEM((WIDTH,), F32),
            pltpu.VMEM((QCOLS,), F32),
            pltpu.VMEM((CHUNKS, HEADS, CW), BF16),
            pltpu.VMEM((2, 2, 8, SUB, CW), BF16),
            pltpu.VMEM((CHUNKS, 2, 8, SUB, CW), BF16),
            pltpu.VMEM((CHUNKS, 2, 8, SUB, CW), BF16),
            pltpu.VMEM((UNITS, 2, 2, SUB, CW), BF16),
            pltpu.VMEM((UNITS, 2, 3, 2, SUB, CW), BF16),
            pltpu.VMEM((2, CHUNKS, SUB, CW), BF16),
            pltpu.VMEM((WQ_SLOTS, 2 * CW, QCOLS), BF16),
            pltpu.VMEM((CHUNKS, rows, CW), BF16),
            pltpu.VMEM((6, 2, HALF, CW), BF16),
            pltpu.VMEM((2, HALF, CW), BF16),
            pltpu.VMEM((2, HALF, CW), BF16),
            pltpu.VMEM((2, 2, 3, HALF, CW), BF16),
            pltpu.VMEM((rows, HEADS), F32),
            pltpu.VMEM((2, 8 * SUB, QCOLS), F32),
            pltpu.VMEM((2, SUB, 1), F32),
            dma((7,)),
            dma((CHUNKS // 2,)),
            dma((WQ_SLOTS,)),
            dma,
            dma((2,)),
            dma((UNITS,)),
            dma,
            dma((UNITS,)),
            dma((UNITS, 2)),
            dma,
            dma,
            dma((CHUNKS, 4)),
            dma((CHUNKS,)),
            dma,
            dma((UNITS, 4)),
            dma,
            dma((2,)),
            dma((2,)),
            dma((2,)),
            dma((2, 2)),
            dma((2,)),
        ],
        compiler_params=pltpu.CompilerParams(
            collective_id=0, has_side_effects=True, vmem_limit_bytes=58 * 2**20
        ),
    )(
        context.reshape(rows, HEADS),
        residual.transpose(0, 2, 1),
        out_weight,
        out_bias,
        norm_gain,
        norm_bias,
        query_weight,
        query_bias,
        grad_handoff.reshape(PIECE, WIDTH),
    )
    query, gctx, gow = pl.pallas_call(
        store,
        out_shape=tuple(jax.ShapeDtypeStruct(shape, BF16) for shape in shapes),
        in_specs=[pl.BlockSpec(memory_space=pltpu.VMEM)] * 3,
        out_specs=(any_spec,) * 3,
        scratch_shapes=[dma((3,))],
        compiler_params=pltpu.CompilerParams(vmem_limit_bytes=4 * 2**20),
    )(*parts)
    return (
        query.reshape(1, SEQ_ROWS, QCOLS),
        gctx.reshape(2, SEQ_ROWS, HEADS),
        gow.reshape(HEADS, CW),
    )


def solution(mesh):
    in_specs = (
        P(None, "dp", ("section", "tensor")),
        P(None, "dp", ("section", "tensor")),
        P(("section", "tensor"), None),
        P(("section", "tensor")),
        P(),
        P(),
        P(None, "tensor"),
        P("tensor"),
        P("section", ("dp", "tensor"), None),
    )
    out_specs = (
        P("section", "dp", "tensor"),
        P(None, "dp", ("section", "tensor")),
        P(("section", "tensor"), "dp"),
    )
    return jax.shard_map(local, mesh=mesh, in_specs=in_specs, out_specs=out_specs, check_vma=False)
```

time: 112 us -> 107 us (0.955)
  Pallas kernels: 110 us -> 106 us
    pallas_call x2, Pallas kernels: 110 us -> 106 us  [the longest x1 105 us: local(): pl.pallas_call(kernel, out_shape=tuple((pltpu.VMEM(shape, BF16) for shape...]
where the time goes in v3:
time: 107 us
  Pallas kernels  106 us (99%)
    pallas_call x1, Pallas kernels, local(): pl.pallas_call(kernel, out_shape=tuple((pltpu.VMEM(shape, BF16) for shape...  105 us

profile of v3, /device:TPU:1, one launch (start us, length us, event | category | flops | bytes accessed | tf_op | source)
XLA Modules:
  0.0 106.7 jit_solution(12377778456820851189)
XLA Ops:
  0.6 104.9 %shard_map.112 = (bf16[8,2,16,768]{3,2,1,0:T(8,128)(2,1)S(1)}, bf16[512,384]{1,0:T(8,128)(2,1)S(1)}, bf16[2,192,1152]{2,1,0:T(8,128)(2,1)S(1)}) custom-call(bf16[512,384]{1,0:T(8,128)(2,1)} %bitcast.8, bf16[2,576,256]{2,1,0:T(8,128)(2,1)} %bitcast.6, bf16[384,9216]{1,0:T(8,128)(2,1)} %ow_hbm.1, f32[576]{0:T(1024)} %bias_hbm.1, f32[9216]{0:T(1024)} %gain_hbm.1, ...), custom_call_target="tpu_custom_call" | custom-call | tf_op jit(solution)/shard_map/pallas_call | solution.py:552
  105.5 1.2 %shard_map.113 = (bf16[8,2,16,768]{3,2,1,0:T(8,128)(2,1)}, bf16[512,384]{1,0:T(8,128)(2,1)}, bf16[2,192,1152]{2,1,0:T(8,128)(2,1)}) custom-call(bf16[8,2,16,768]{3,2,1,0:T(8,128)(2,1)S(1)} %get-tuple-element.9.refs_0_, bf16[512,384]{1,0:T(8,128)(2,1)S(1)} %get-tuple-element.10.refs_1_, bf16[2,192,1152]{2,1,0:T(8,128)(2,1)S(1)} %get-tuple-element.11.refs_2_), custom_call_target="tpu_custom_call" | custom-call | tf_op jit(solution)/shard_map/pallas_call | solution.py:620
